TPU v7x, 32 devices: a whole 2x2x4 slice. The times are simulated.
32 devices in a mesh: dp: 8 (over z, x), tensor: 4 (over y, core).
Axes of the slice: x: 2, y: 2, z: 4, core: 2. Of those that a mesh axis runs over, the one named last changes fastest.
Arguments:
- layer_input: bfloat16 [4096, 768], P(('dp', 'tensor')), may hold values from -6 to 6
- seq_lengths: int32 [8, 3], P('dp'), may hold values from 1 to 480, 512 in all within a row
- expert_ids: int32 [4096, 1], P('dp'), may hold values from 0 to 7; in each aligned block of 512 rows (0 to 511, 512 to 1023, ...) at most 65 rows name the same one
- bucket_table: int32 [959], replicated, may hold values from 0 to 31, as said below
- gain_attn: bfloat16 [768], replicated, may hold values from 0.5 to 1.5
- gain_moe: bfloat16 [768], replicated, may hold values from 0.5 to 1.5
- w_query: bfloat16 [768, 768], P('dp', 'tensor'), may hold values from -0.21875 to 0.21875
- w_key: bfloat16 [768, 768], P('dp', 'tensor'), may hold values from -0.21875 to 0.21875
- w_value: bfloat16 [768, 768], P('dp', 'tensor'), may hold values from -0.21875 to 0.21875
- w_attn_out: bfloat16 [768, 768], P('tensor', 'dp'), may hold values from -3 to 3
- w_router: bfloat16 [768, 8], P('dp'), may hold values from -0.109375 to 0.109375
- rel_bias: bfloat16 [32, 12], P(None, 'tensor'), may hold values from -4 to 4
- w_in: bfloat16 [8, 768, 3072], P('dp', None, 'tensor'), may hold values from -0.21875 to 0.21875
- w_out: bfloat16 [8, 3072, 768], P('dp', 'tensor'), may hold values from -4 to 4
- cotangent: bfloat16 [4096, 768], P(('dp', 'tensor')), may hold values from -6 to 6
Outputs:
- layer_output: bfloat16 [4096, 768], P(('dp', 'tensor'))
- grad_input: float32 [4096, 768], P(('dp', 'tensor'))
- grad_gain_attn: float32 [768], replicated
- grad_gain_moe: float32 [768], replicated
- grad_query: float32 [768, 768], P('dp', 'tensor')
- grad_key: float32 [768, 768], P('dp', 'tensor')
- grad_value: float32 [768, 768], P('dp', 'tensor')
- grad_attn_out: float32 [768, 768], P('tensor', 'dp')
- grad_router: float32 [768, 8], P('dp')
- grad_rel_bias: float32 [32, 12], P(None, 'tensor')
- grad_w_in: float32 [8, 768, 3072], P('dp', None, 'tensor')
- grad_w_out: float32 [8, 3072, 768], P('dp', 'tensor')
Inputs may be any that keep to these rules, and one draw needn't show every extreme that they name: `seq_lengths`: row g lists the lengths of the sequences packed, in order, into the 512 tokens of group g; each row sums to 512. `expert_ids`: within the 512 tokens of one group no expert is named by more than 65 tokens. `bucket_table`: entry r is the bucket of the relative position r - 480 + 1 (key position minus query position); it depends only on that position.
All inputs are finite; a program needn't handle non-finite values.
Results may differ from a plain program's by a relative error of at most 0.025.
Values may be sent and summed in bfloat16 or wider, within the bound.
A program may use at most 128 MiB of HBM per device.

v0:
```python
import jax
import jax.numpy as jnp
from jax import lax
from jax.sharding import PartitionSpec as P

DH = 64


EPS = 1e-06
NEG_FILL = -1e30


def seq_gather(operand):
    return lax.all_gather(operand, "tensor", axis=0, tiled=True)


def seq_scatter(operand):
    return lax.psum_scatter(
        operand.astype(jnp.bfloat16), "tensor", scatter_dimension=0, tiled=True
    ).astype(jnp.float32)


def send_experts(operand):
    return lax.all_to_all(operand, "dp", split_axis=0, concat_axis=0, tiled=True)


def rounded(operand):
    return lax.optimization_barrier(operand.astype(jnp.bfloat16)).astype(jnp.float32)


def unchanged(operand):
    return operand


def return_rows(partial_value, destination, finish, groups, capacity):
    width = partial_value.shape[-1]
    arrived = lax.all_to_all(
        partial_value.reshape(groups, capacity, width).astype(jnp.bfloat16),
        "dp",
        split_axis=0,
        concat_axis=0,
        tiled=True,
    ).astype(jnp.float32)
    picked = arrived.reshape(-1, width)[destination]
    return finish(seq_scatter(picked))


def contract_rows(left, right):
    return lax.dot_general(
        left, right, (((0,), (0,)), ((), ())), preferred_element_type=jnp.float32
    )


def contract_cols(left, right):
    return lax.dot_general(
        left, right, (((1,), (1,)), ((), ())), preferred_element_type=jnp.float32
    )


def norm_back(grad_norm, unit_rows, inv_rms, gain):
    scaled = grad_norm * gain
    return inv_rms * (scaled - unit_rows * jnp.mean(scaled * unit_rows, axis=-1, keepdims=True))


def expand_diagonals(line_vals, num_rows, num_keys):
    heads, length = line_vals.shape
    rolled = jnp.roll(line_vals, -(num_rows - 1), axis=1)
    tiled = jnp.tile(rolled, (1, num_rows))
    return tiled[:, : num_rows * (length - 1)].reshape(heads, num_rows, length - 1)[:, :, :num_keys]


def diagonal_sums(grid):
    heads, num_rows, num_keys = grid.shape
    flipped = grid[:, ::-1, :]
    padded = jnp.pad(flipped, ((0, 0), (0, 0), (0, num_rows)))
    flat_rows = padded.reshape(heads, num_rows * (num_keys + num_rows))[
        :, : num_rows * (num_keys + num_rows - 1)
    ]
    return jnp.sum(flat_rows.reshape(heads, num_rows, num_keys + num_rows - 1), axis=1)


def shards(
    layer_input,
    seq_lengths,
    expert_ids,
    bucket_table,
    gain_attn,
    gain_moe,
    w_query,
    w_key,
    w_value,
    w_attn_out,
    w_router,
    rel_bias,
    w_in,
    w_out,
    cotangent,
):
    float_type = jnp.float32
    half_type = jnp.bfloat16
    tok_dev, width = layer_input.shape
    group_tok = expert_ids.shape[0]
    experts = w_router.shape[1]
    capacity = group_tok // experts + 1
    local_heads = rel_bias.shape[1]
    head_cols = local_heads * DH
    max_length = (bucket_table.shape[0] + 1) // 2
    buckets = rel_bias.shape[0]
    tensor_rank = lax.axis_index("tensor")
    row_offset = tensor_rank * tok_dev
    score_scale = DH ** (-0.5)
    places = jnp.arange(group_tok, dtype=jnp.int32)
    seq_lens = seq_lengths[0]
    seq_starts = jnp.cumsum(seq_lens) - seq_lens
    segment = jnp.sum((places[:, None] >= seq_starts[None, :]).astype(jnp.int32), axis=1) - 1
    bucket_hot = (bucket_table[:, None] == jnp.arange(buckets, dtype=jnp.int32)[None, :]).astype(
        float_type
    )
    rel_table = jnp.dot(bucket_hot, rel_bias.astype(float_type), precision=lax.Precision.HIGHEST).T
    query_all, key_all, value_all, router_all = (
        lax.all_gather(w_query, "dp", axis=0, tiled=True),
        lax.all_gather(w_key, "dp", axis=0, tiled=True),
        lax.all_gather(w_value, "dp", axis=0, tiled=True),
        lax.all_gather(w_router, "dp", axis=0, tiled=True),
    )
    out_all = lax.all_gather(w_attn_out, "dp", axis=1, tiled=True)
    input_f = layer_input.astype(float_type)
    gain_one = gain_attn.astype(float_type)
    inv_one = lax.rsqrt(jnp.mean(input_f * input_f, axis=-1, keepdims=True) + EPS)
    unit_one = input_f * inv_one
    normed_one = (unit_one * gain_one).astype(half_type)
    full_one = seq_gather(normed_one)
    queries = (
        jnp.dot(full_one, query_all, preferred_element_type=float_type)
        .astype(half_type)
        .reshape(group_tok, local_heads, DH)
    )
    keys_loc = (
        jnp.dot(full_one, key_all, preferred_element_type=float_type)
        .astype(half_type)
        .reshape(group_tok, local_heads, DH)
    )
    values_loc = (
        jnp.dot(full_one, value_all, preferred_element_type=float_type)
        .astype(half_type)
        .reshape(group_tok, local_heads, DH)
    )
    num_blocks = max(1, group_tok // 512)
    block_rows = group_tok // num_blocks
    line_len = group_tok + block_rows - 1
    line_places = jnp.arange(line_len, dtype=jnp.int32)

    def block_lines(offset):
        return jnp.clip(
            line_places - (block_rows - 1) - offset + max_length - 1, 0, 2 * max_length - 2
        )

    def block_scores(offset):
        raw = (
            jnp.einsum("qhd,khd->hqk", queries, keys_loc, preferred_element_type=float_type)
            * score_scale
        )
        line_index = block_lines(offset)
        raw = raw + expand_diagonals(rel_table[:, line_index], block_rows, group_tok)
        same_seq = segment[:, None] == segment[None, :]
        return (jnp.where(same_seq[None], raw, NEG_FILL), line_index)

    number = 0
    offset = number * block_rows
    scores, line_index = block_scores(offset)
    row_max = jnp.max(scores, axis=-1, keepdims=True)
    expo = jnp.exp(scores - row_max)
    row_total = jnp.sum(expo, axis=-1, keepdims=True)
    weights_row = (expo / row_total).astype(half_type)
    head_parts = jnp.einsum(
        "hqk,khd->qhd", weights_row, values_loc, preferred_element_type=float_type
    ).astype(half_type)
    lse_parts = [row_max + jnp.log(row_total)]
    head_out = head_parts.reshape(group_tok, head_cols)
    attn_rows = seq_scatter(jnp.dot(head_out, out_all, preferred_element_type=float_type))
    mixed = input_f + attn_rows
    gain_two = gain_moe.astype(float_type)
    inv_two = lax.rsqrt(jnp.mean(mixed * mixed, axis=-1, keepdims=True) + EPS)
    unit_two = mixed * inv_two
    normed_two = (unit_two * gain_two).astype(half_type)
    full_two = seq_gather(normed_two)
    logits = jnp.dot(normed_two, router_all, preferred_element_type=float_type)
    router_prob = jax.nn.softmax(logits, axis=-1)
    expert_row = expert_ids[:, 0]
    one_hot = (expert_row[:, None] == jnp.arange(experts, dtype=jnp.int32)[None, :]).astype(
        jnp.int32
    )
    slot_index = jnp.sum((jnp.cumsum(one_hot, axis=0) - one_hot) * one_hot, axis=1)
    destination = expert_row * capacity + slot_index
    own_choice = lax.dynamic_slice_in_dim(one_hot, row_offset, tok_dev, 0).astype(float_type)
    gate_prob = jnp.sum(router_prob * own_choice, axis=1, keepdims=True)
    buffer = jnp.zeros((experts * capacity, width), half_type).at[destination].set(full_two)
    arrived = send_experts(buffer.reshape(experts, capacity, width)).reshape(-1, width)
    hidden = jnp.dot(arrived, w_in[0], preferred_element_type=float_type)
    activated = jax.nn.gelu(hidden, approximate=False).astype(half_type)
    partial_value = jnp.dot(activated, w_out[0], preferred_element_type=float_type)
    expert_y = return_rows(partial_value, destination, rounded, experts, capacity)
    layer_output = (mixed + gate_prob * expert_y).astype(half_type)
    grad_out = cotangent.astype(float_type)
    grad_gate = jnp.sum(grad_out * expert_y, axis=1, keepdims=True)
    grad_y = (gate_prob * grad_out).astype(half_type)
    grad_y_full = seq_gather(grad_y)
    grad_buffer = jnp.zeros((experts * capacity, width), half_type).at[destination].set(grad_y_full)
    grad_arrived = send_experts(grad_buffer.reshape(experts, capacity, width)).reshape(-1, width)
    grad_w_out = contract_rows(activated, grad_arrived)
    grad_act = contract_cols(grad_arrived, w_out[0])
    grad_hidden = jax.vjp(lambda operand: jax.nn.gelu(operand, approximate=False), hidden)[1](
        grad_act
    )[0].astype(half_type)
    grad_w_in = contract_rows(arrived, grad_hidden)
    grad_rows = contract_cols(grad_hidden, w_in[0])
    grad_norm_two = return_rows(grad_rows, destination, unchanged, experts, capacity)
    grad_logits = (router_prob * (own_choice - gate_prob) * grad_gate).astype(half_type)
    grad_router = contract_rows(normed_two, grad_logits)
    grad_norm_two = grad_norm_two + contract_cols(grad_logits, router_all)
    gain_two_part = jnp.sum(grad_norm_two * unit_two, axis=0)
    grad_mixed = grad_out + norm_back(grad_norm_two, unit_two, inv_two, gain_two)
    grad_attn_full = seq_gather(grad_mixed.astype(half_type))
    grad_out_proj = contract_rows(head_out, grad_attn_full)
    grad_heads = (
        contract_cols(grad_attn_full, out_all).astype(half_type).reshape(group_tok, local_heads, DH)
    )
    bucket_range = jnp.arange(buckets, dtype=jnp.int32)
    number = 0
    offset = number * block_rows
    scores, line_index = block_scores(offset)
    prob_full = jnp.exp(scores - lse_parts[number])
    prob_low = prob_full.astype(half_type)
    grad_values = jnp.einsum(
        "hqk,qhd->khd", prob_low, grad_heads, preferred_element_type=float_type
    )
    grad_prob = jnp.einsum(
        "qhd,khd->hqk", grad_heads, values_loc, preferred_element_type=float_type
    )
    grad_scores = (
        prob_full * (grad_prob - jnp.sum(prob_full * grad_prob, axis=-1, keepdims=True))
    ).astype(half_type)
    query_grads = (
        jnp.einsum("hqk,khd->qhd", grad_scores, keys_loc, preferred_element_type=float_type)
        * score_scale
    )
    grad_keys = (
        jnp.einsum("hqk,qhd->khd", grad_scores, queries, preferred_element_type=float_type)
        * score_scale
    )
    line_sums = diagonal_sums(grad_scores.astype(float_type))
    line_hot = (bucket_table[line_index][:, None] == bucket_range[None, :]).astype(float_type)
    grad_bucket = jnp.dot(line_sums, line_hot, precision=lax.Precision.HIGHEST)
    grad_queries = query_grads.reshape(group_tok, head_cols).astype(half_type)
    grad_keys = grad_keys.reshape(group_tok, head_cols).astype(half_type)
    grad_values = grad_values.reshape(group_tok, head_cols).astype(half_type)
    grad_query_full = contract_rows(full_one, grad_queries)
    grad_key_full = contract_rows(full_one, grad_keys)
    grad_value_full = contract_rows(full_one, grad_values)
    grad_full_one = (
        contract_cols(grad_queries, query_all)
        + contract_cols(grad_keys, key_all)
        + contract_cols(grad_values, value_all)
    )
    grad_norm_one = seq_scatter(grad_full_one)
    gain_one_part = jnp.sum(grad_norm_one * unit_one, axis=0)
    grad_input = grad_mixed + norm_back(grad_norm_one, unit_one, inv_one, gain_one)
    bias_local = grad_bucket.T
    bias_full = jnp.zeros((buckets, local_heads * lax.axis_size("tensor")), float_type)
    bias_full = lax.dynamic_update_slice_in_dim(bias_full, bias_local, tensor_rank * local_heads, 1)
    grad_query, grad_key, grad_value = (
        lax.psum_scatter(grad_query_full, "dp", scatter_dimension=0, tiled=True),
        lax.psum_scatter(grad_key_full, "dp", scatter_dimension=0, tiled=True),
        lax.psum_scatter(grad_value_full, "dp", scatter_dimension=0, tiled=True),
    )
    grad_attn_out = lax.psum_scatter(grad_out_proj, "dp", scatter_dimension=1, tiled=True)
    gain_one_sum, gain_two_sum, bias_sum, router_sum = lax.psum(
        (gain_one_part, gain_two_part, bias_full, grad_router), ("dp", "tensor")
    )
    router_rows = w_router.shape[0]
    grad_router_rows = lax.dynamic_slice_in_dim(
        router_sum, lax.axis_index("dp") * router_rows, router_rows, 0
    )
    grad_bias_cols = lax.dynamic_slice_in_dim(bias_sum, tensor_rank * local_heads, local_heads, 1)
    return (
        layer_output,
        grad_input,
        gain_one_sum,
        gain_two_sum,
        grad_query,
        grad_key,
        grad_value,
        grad_attn_out,
        grad_router_rows,
        grad_bias_cols,
        grad_w_in[None],
        grad_w_out[None],
    )


def solution(mesh):
    return jax.shard_map(
        shards,
        mesh=mesh,
        in_specs=(
            P(("dp", "tensor"), None),
            P("dp", None),
            P("dp", None),
            P(),
            P(),
            P(),
            P("dp", "tensor"),
            P("dp", "tensor"),
            P("dp", "tensor"),
            P("tensor", "dp"),
            P("dp", None),
            P(None, "tensor"),
            P("dp", None, "tensor"),
            P("dp", "tensor", None),
            P(("dp", "tensor"), None),
        ),
        out_specs=(
            P(("dp", "tensor"), None),
            P(("dp", "tensor"), None),
            P(),
            P(),
            P("dp", "tensor"),
            P("dp", "tensor"),
            P("dp", "tensor"),
            P("tensor", "dp"),
            P("dp", None),
            P(None, "tensor"),
            P("dp", None, "tensor"),
            P("dp", "tensor", None),
        ),
        check_vma=False,
    )
```

profile of v0, /device:TPU:0, one launch (start us, length us, event | category | flops | bytes accessed | tf_op | source)
XLA Modules:
  0.0 734.6 jit_solution(2782952510032259147)
XLA Ops:
  13.8 32.9 %all_gather.31 = bf16[192,768]{0,1:T(8,128)(2,1)S(1)} all-gather(bf16[192,96]{0,1:T(8,128)(2,1)S(1)} %copy.58), channel_id=1, replica_groups=mesh['dp'=8,'tensor'=4] {'dp'}, dimensions={1}, use_global_device_ids=true | all-gather | bytes 331776 | tf_op jit(solution)/shard_map/all_gather | solution.py:126
  46.7 31.0 %all_gather.29 = bf16[768,192]{1,0:T(8,128)(2,1)S(1)} all-gather(bf16[96,192]{1,0:T(8,128)(2,1)S(1)} %copy-done.57), channel_id=1, replica_groups=mesh['dp'=8,'tensor'=4] {'dp'}, dimensions={0}, use_global_device_ids=true | all-gather | bytes 331776 | tf_op jit(solution)/shard_map/all_gather | solution.py:121
  77.6 31.0 %all_gather.30 = bf16[768,192]{1,0:T(8,128)(2,1)S(1)} all-gather(bf16[96,192]{1,0:T(8,128)(2,1)S(1)} %copy-done.58), channel_id=1, replica_groups=mesh['dp'=8,'tensor'=4] {'dp'}, dimensions={0}, use_global_device_ids=true | all-gather | bytes 331776 | tf_op jit(solution)/shard_map/all_gather | solution.py:122
  108.7 31.1 %all_gather.28 = bf16[768,192]{1,0:T(8,128)(2,1)S(1)} all-gather(bf16[96,192]{1,0:T(8,128)(2,1)S(1)} %copy-done.59), channel_id=1, replica_groups=mesh['dp'=8,'tensor'=4] {'dp'}, dimensions={0}, use_global_device_ids=true | all-gather | bytes 331776 | tf_op jit(solution)/shard_map/all_gather | solution.py:123
  141.3 8.6 %all_gather.27 = bf16[512,768]{1,0:T(8,128)(2,1)S(1)} all-gather(bf16[128,768]{1,0:T(8,128)(2,1)S(1)} %fusion.40), channel_id=1, replica_groups=mesh['dp'=8,'tensor'=4] {'tensor'}, dimensions={0}, use_global_device_ids=true | all-gather | bytes 983040 | tf_op jit(solution)/shard_map/all_gather | solution.py:14
  154.7 13.4 %tile.5 = f32[3,523776]{1,0:T(4,128)} reshape(f32[3,512,1023]{2,1,0:T(8,128)} %tile.4) | data formatting | bytes 12570624 | tf_op jit(solution)/shard_map/tile | solution.py:68
  168.1 7.6 %slice.44 = f32[3,523264]{1,0:T(4,128)} slice(f32[3,523776]{1,0:T(4,128)} %tile.5), slice={[0:3], [0:523264]} | slice | bytes 12558336 | tf_op jit(solution)/shard_map/slice | solution.py:69
  175.8 13.3 %reshape.209 = f32[3,512,1022]{2,1,0:T(8,128)} reshape(f32[3,523264]{1,0:T(4,128)} %slice.44) | data formatting | bytes 12558336 | tf_op jit(solution)/shard_map/reshape | solution.py:69
  189.1 3.9 slice.45
  203.9 21.9 %reduce-scatter.11.cloned.1.call-done = bf16[128,768]{1,0:T(8,128)(2,1)} async-done(((bf16[512,768]{1,0:T(8,128)(2,1)}), bf16[128,768]{1,0:T(8,128)(2,1)}) %reduce-scatter.11.cloned.1.call-update) | async-done | bytes 196624 | tf_op jit(solution)/shard_map/reduce_scatter | solution.py:18
  228.0 8.2 %all_gather.33 = bf16[512,768]{1,0:T(8,128)(2,1)S(1)} all-gather(bf16[128,768]{1,0:T(8,128)(2,1)S(1)} %multiply_convert_fusion.2), channel_id=1, replica_groups=mesh['dp'=8,'tensor'=4] {'tensor'}, dimensions={0}, use_global_device_ids=true | all-gather | bytes 983040 | tf_op jit(solution)/shard_map/all_gather | solution.py:14
  239.8 28.5 %all_to_all.20 = bf16[8,65,768]{2,1,0:T(8,128)(2,1)S(1)} all-to-all(bf16[8,65,768]{2,1,0:T(8,128)(2,1)S(1)} %reshape.212), channel_id=1, replica_groups=mesh['dp'=8,'tensor'=4] {'dp'}, dimensions={0} | all-to-all | bytes 1597440 | tf_op jit(solution)/shard_map/all_to_all | solution.py:24
  268.5 5.4 multiply_convert_fusion.1
  280.9 21.9 %all-to-all-done.1 = bf16[8,65,768]{2,1,0:T(8,128)(2,1)S(1)} async-done(((bf16[8,65,768]{2,1,0:T(8,128)(2,1)}), bf16[8,65,768]{2,1,0:T(8,128)(2,1)S(1)}, u32[]{:S(2)}, u32[]{:S(2)}) %all-to-all-start.1) | async-done | bytes 798752 | tf_op jit(solution)/shard_map/all_to_all | solution.py:37
  305.8 26.0 %all-gather = bf16[8,96,8]{1,2,0:T(8,128)(2,1)S(1)} all-gather(bf16[1,96,8]{1,2,0:T(8,128)(2,1)S(1)} %bitcast.141), channel_id=1, replica_groups=mesh['dp'=8,'tensor'=4] {'dp'}, dimensions={0}, use_global_device_ids=true | all-gather | bytes 13824 | tf_op jit(solution)/shard_map/all_gather | solution.py:124
  333.3 8.1 %all_gather.34 = bf16[512,768]{1,0:T(8,128)(2,1)S(1)} all-gather(bf16[128,768]{1,0:T(8,128)(2,1)S(1)} %get-tuple-element.24), channel_id=1, replica_groups=mesh['dp'=8,'tensor'=4] {'tensor'}, dimensions={0}, use_global_device_ids=true | all-gather | bytes 983040 | tf_op jit(solution)/shard_map/all_gather | solution.py:14
  344.5 26.1 %all_to_all.21 = bf16[8,65,768]{2,1,0:T(8,128)(2,1)S(1)} all-to-all(bf16[8,65,768]{2,1,0:T(8,128)(2,1)S(1)} %reshape.216), channel_id=1, replica_groups=mesh['dp'=8,'tensor'=4] {'dp'}, dimensions={0} | all-to-all | bytes 1597440 | tf_op jit(solution)/shard_map/all_to_all | solution.py:24
  370.9 3.6 add_convert_fusion
  378.6 25.9 %all_to_all.22 = bf16[8,65,768]{2,1,0:T(8,128)(2,1)S(1)} all-to-all(bf16[8,65,768]{2,1,0:T(8,128)(2,1)S(1)} %convolution_convert_fusion), channel_id=1, replica_groups=mesh['dp'=8,'tensor'=4] {'dp'}, dimensions={0} | all-to-all | bytes 1597440 | tf_op jit(solution)/shard_map/all_to_all | solution.py:37
  407.6 21.5 %reduce-scatter.15.cloned.1.call-done = bf16[128,768]{1,0:T(8,128)(2,1)} async-done(((bf16[512,768]{1,0:T(8,128)(2,1)}), bf16[128,768]{1,0:T(8,128)(2,1)}) %reduce-scatter.15.cloned.1.call-update) | async-done | bytes 196624 | tf_op jit(solution)/shard_map/reduce_scatter | solution.py:18
  431.3 8.2 %all_gather.35 = bf16[512,768]{1,0:T(8,128)(2,1)S(1)} all-gather(bf16[128,768]{1,0:T(8,128)(2,1)S(1)} %fusion.55), channel_id=1, replica_groups=mesh['dp'=8,'tensor'=4] {'tensor'}, dimensions={0}, use_global_device_ids=true | all-gather | bytes 983040 | tf_op jit(solution)/shard_map/all_gather | solution.py:14
  454.6 4.7 gather_fusion.3
  465.4 17.4 %rev.3 = f32[3,512,512]{1,2,0:T(8,128)} reverse(bf16[3,512,512]{1,2,0:T(8,128)(2,1)S(1)} %copy-done.8), dimensions={1} | reverse | bytes 4718592 | tf_op jit(solution)/shard_map/rev | solution.py:74
  487.7 5.4 pad_bitcast_fusion
  493.1 7.1 copy.72
  500.2 4.4 slice.47
  504.6 13.2 %reshape.222 = f32[3,512,1023]{2,1,0:T(8,128)} reshape(f32[3,523776]{1,0:T(4,128)} %slice.47) | data formatting | bytes 12570624 | tf_op jit(solution)/shard_map/reshape | solution.py:79
  523.4 6.3 reduce-scatter.17.cloned.1.call-done
  530.9 40.5 %all-reduce.1 = (f32[768]{0:T(1024)}, f32[768]{0:T(1024)}, f32[768,8]{0,1:T(8,128)S(1)}, f32[32,12]{0,1:T(8,128)S(1)}) all-reduce(f32[768]{0:T(1024)S(1)} %get-tuple-element.14, f32[768]{0:T(1024)S(1)} %get-tuple-element.12, f32[768,8]{0,1:T(8,128)S(1)} %fusion.59, ...), channel_id=1, replica_groups=mesh['dp'=8,'tensor'=4] {'dp','tensor'}, use_global_device_ids=true, to_apply=%region_23.24 | all-reduce | flops 8064 | bytes 64512 | tf_op jit(solution)/shard_map/psum | solution.py:277
  574.6 21.7 %reduce-scatter.23.cloned.1.call-done = f32[96,192]{1,0:T(8,128)} async-done(((f32[768,192]{1,0:T(8,128)}), f32[96,192]{1,0:T(8,128)}) %reduce-scatter.23.cloned.1.call-update) | async-done | bytes 73744 | tf_op jit(solution)/shard_map/reduce_scatter | solution.py:274
  596.3 65.3 %reduce-scatter.21.cloned.1.call-done = f32[96,192]{1,0:T(8,128)} async-done(((f32[768,192]{1,0:T(8,128)}), f32[96,192]{1,0:T(8,128)}) %reduce-scatter.21.cloned.1.call-update) | async-done | bytes 73744 | tf_op jit(solution)/shard_map/reduce_scatter | solution.py:273
  661.6 65.7 %reduce-scatter.19.cloned.1.call-done = f32[96,192]{1,0:T(8,128)} async-done(((f32[768,192]{1,0:T(8,128)}), f32[96,192]{1,0:T(8,128)}) %reduce-scatter.19.cloned.1.call-update) | async-done | bytes 73744 | tf_op jit(solution)/shard_map/reduce_scatter | solution.py:272
  (286 shorter events, 89.0 us)
Async XLA Ops:
  7.2 261.3 %copy-start = (bf16[1,768,768]{2,1,0:T(8,128)(2,1)S(1)}, bf16[1,768,768]{2,1,0:T(8,128)(2,1)}, u32[]{:S(2)}) copy-start(bf16[1,768,768]{2,1,0:T(8,128)(2,1)} %param.27) | copy-start | bytes 3538948
  7.2 39.4 %copy-start.57 = (bf16[96,192]{1,0:T(8,128)(2,1)S(1)}, bf16[96,192]{1,0:T(8,128)(2,1)}, u32[]{:S(2)}) copy-start(bf16[96,192]{1,0:T(8,128)(2,1)} %param.21) | copy-start | bytes 110596
  7.2 218.6 %reduce-scatter.11.cloned.1.call-start = ((), (), s32[]{:S(2)}) async-start(), calls=%async_computation.12 | async-start | bytes 983040 | tf_op jit(solution)/shard_map/reduce_scatter | solution.py:18
  7.3 70.3 %copy-start.64 = (s32[1024]{0:T(1024)}, s32[1024]{0:T(1024)S(1)}, u32[]{:S(2)}) copy-start(s32[1024]{0:T(1024)S(1)} %pad_clamp_fusion.1) | copy-start | bytes 12292
  8.5 69.1 %copy-start.58 = (bf16[96,192]{1,0:T(8,128)(2,1)S(1)}, bf16[96,192]{1,0:T(8,128)(2,1)}, u32[]{:S(2)}) copy-start(bf16[96,192]{1,0:T(8,128)(2,1)} %param.22) | copy-start | bytes 110596
  8.7 100.0 %copy-start.59 = (bf16[96,192]{1,0:T(8,128)(2,1)S(1)}, bf16[96,192]{1,0:T(8,128)(2,1)}, u32[]{:S(2)}) copy-start(bf16[96,192]{1,0:T(8,128)(2,1)} %param.23) | copy-start | bytes 110596
  12.6 137.3 %copy-start.74 = (f32[128]{0:T(128)}, f32[128]{0:T(128)S(1)}, u32[]{:S(2)}) copy-start(f32[128]{0:T(128)S(1)} %add_rsqrt_fusion.1) | copy-start | bytes 1540
  12.7 137.2 %copy-start.49 = (f32[768]{0:T(1024)}, f32[768]{0:T(1024)S(1)}, u32[]{:S(2)}) copy-start(f32[768]{0:T(1024)S(1)} %convert_element_type.146) | copy-start | bytes 9220
  46.6 154.4 %copy-start.12 = (bf16[192,768]{0,1:T(8,128)(2,1)}, bf16[192,768]{0,1:T(8,128)(2,1)S(1)}, u32[]{:S(2)}) copy-start(bf16[192,768]{0,1:T(8,128)(2,1)S(1)} %all_gather.31) | copy-start | bytes 884740
  77.6 72.7 %copy-start.14 = (bf16[768,192]{1,0:T(8,128)(2,1)}, bf16[768,192]{1,0:T(8,128)(2,1)S(1)}, u32[]{:S(2)}) copy-start(bf16[768,192]{1,0:T(8,128)(2,1)S(1)} %all_gather.29) | copy-start | bytes 884740
  108.7 41.7 %copy-start.16 = (bf16[768,192]{1,0:T(8,128)(2,1)}, bf16[768,192]{1,0:T(8,128)(2,1)S(1)}, u32[]{:S(2)}) copy-start(bf16[768,192]{1,0:T(8,128)(2,1)S(1)} %all_gather.30) | copy-start | bytes 884740
  150.3 46.2 %copy-start.30 = (bf16[512,192]{0,1:T(8,128)(2,1)}, bf16[512,192]{0,1:T(8,128)(2,1)S(1)}, u32[]{:S(2)}) copy-start(bf16[512,192]{0,1:T(8,128)(2,1)S(1)} %convolution_convert_fusion.4) | copy-start | bytes 589828
  150.8 45.8 %copy-start.32 = (bf16[512,192]{0,1:T(8,128)(2,1)}, bf16[512,192]{0,1:T(8,128)(2,1)S(1)}, u32[]{:S(2)}) copy-start(bf16[512,192]{0,1:T(8,128)(2,1)S(1)} %convolution_convert_fusion.5) | copy-start | bytes 589828
  151.2 48.6 %copy-start.45 = (bf16[512,192]{0,1:T(8,128)(2,1)}, bf16[512,192]{0,1:T(8,128)(2,1)S(1)}, u32[]{:S(2)}) copy-start(bf16[512,192]{0,1:T(8,128)(2,1)S(1)} %convolution_convert_fusion.6) | copy-start | bytes 589828
  228.0 103.9 %copy-start.19 = (bf16[128,768]{1,0:T(8,128)(2,1)}, bf16[128,768]{1,0:T(8,128)(2,1)S(1)}, u32[]{:S(2)}) copy-start(bf16[128,768]{1,0:T(8,128)(2,1)S(1)} %multiply_convert_fusion.2) | copy-start | bytes 589828
  277.2 25.5 %all-to-all-start.1 = ((bf16[8,65,768]{2,1,0:T(8,128)(2,1)}), bf16[8,65,768]{2,1,0:T(8,128)(2,1)S(1)}, u32[]{:S(2)}, u32[]{:S(2)}) async-start(bf16[8,65,768]{2,1,0:T(8,128)(2,1)} %convolution_convert_fusion.1), calls=%async_computation.2 | async-start | bytes 1769472 | tf_op jit(solution)/shard_map/all_to_all | solution.py:37
  280.8 51.4 %reduce-scatter.13.cloned.1.call-start = ((), (), s32[]{:S(2)}) async-start(), calls=%async_computation.13 | async-start | bytes 983040 | tf_op jit(solution)/shard_map/reduce_scatter | solution.py:18
  305.7 123.4 %reduce-scatter.15.cloned.1.call-start = ((), (), s32[]{:S(2)}) async-start(), calls=%async_computation.14 | async-start | bytes 983040 | tf_op jit(solution)/shard_map/reduce_scatter | solution.py:18
  332.2 97.0 %copy-start.76 = (f32[128]{0:T(128)}, f32[128]{0:T(128)S(1)}, u32[]{:S(2)}) copy-start(f32[128]{0:T(128)S(1)} %fusion.54) | copy-start | bytes 1540
  332.2 96.9 %copy-start.69 = (f32[128]{0:T(128)}, f32[128]{0:T(128)S(1)}, u32[]{:S(2)}) copy-start(f32[128]{0:T(128)S(1)} %multiply_reduce_fusion.4) | copy-start | bytes 1540
  333.3 95.8 %copy-start.81 = (f32[128]{0:T(128)}, f32[128]{0:T(128)S(1)}, u32[]{:S(2)}) copy-start(f32[128]{0:T(128)S(1)} %get-tuple-element.25) | copy-start | bytes 1540
  407.6 114.1 %reduce-scatter.25.cloned.1.call-start = ((), (), s32[]{:S(2)}) async-start(), calls=%async_computation.19 | async-start | bytes 884736
  442.0 87.6 %reduce-scatter.17.cloned.1.call-start = ((), (), s32[]{:S(2)}) async-start(), calls=%async_computation.15 | async-start | bytes 983040 | tf_op jit(solution)/shard_map/reduce_scatter | solution.py:18
  450.7 145.6 %reduce-scatter.23.cloned.1.call-start = ((), (), s32[]{:S(2)}) async-start(), calls=%async_computation.18 | async-start | bytes 884736 | tf_op jit(solution)/shard_map/reduce_scatter | solution.py:274
  453.0 208.6 %reduce-scatter.21.cloned.1.call-start = ((), (), s32[]{:S(2)}) async-start(), calls=%async_computation.17 | async-start | bytes 884736 | tf_op jit(solution)/shard_map/reduce_scatter | solution.py:273
  454.5 272.8 %reduce-scatter.19.cloned.1.call-start = ((), (), s32[]{:S(2)}) async-start(), calls=%async_computation.16 | async-start | bytes 884736 | tf_op jit(solution)/shard_map/reduce_scatter | solution.py:272
  517.8 54.8 %copy-start.25 = (bf16[128,768]{1,0:T(8,128)(2,1)S(1)}, bf16[128,768]{1,0:T(8,128)(2,1)}, u32[]{:S(2)}) copy-start(bf16[128,768]{1,0:T(8,128)(2,1)} %param.29) | copy-start | bytes 589828
  517.8 54.8 %copy-start.35 = (f32[128,768]{1,0:T(8,128)S(1)}, f32[128,768]{1,0:T(8,128)}, u32[]{:S(2)}) copy-start(f32[128,768]{1,0:T(8,128)} %copy-done.34) | copy-start | bytes 1179652
  517.8 54.8 %copy-start.46 = (bf16[128,768]{1,0:T(8,128)(2,1)S(1)}, bf16[128,768]{1,0:T(8,128)(2,1)}, u32[]{:S(2)}) copy-start(bf16[128,768]{1,0:T(8,128)(2,1)} %reduce-scatter.13.cloned.1.call-done) | copy-start | bytes 589828
  517.8 54.8 %copy-start.53 = (f32[768]{0:T(1024)S(1)}, f32[768]{0:T(1024)}, u32[]{:S(2)}) copy-start(f32[768]{0:T(1024)} %copy-done.51) | copy-start | bytes 9220
  517.8 54.8 %copy-start.80 = (f32[128]{0:T(128)S(1)}, f32[128]{0:T(128)}, u32[]{:S(2)}) copy-start(f32[128]{0:T(128)} %copy-done.78) | copy-start | bytes 1540
  517.8 209.5 %copy-start.1 = (bf16[1,768,768]{2,1,0:T(8,128)(2,1)S(1)}, bf16[1,768,768]{2,1,0:T(8,128)(2,1)}, u32[]{:S(2)}) copy-start(bf16[1,768,768]{2,1,0:T(8,128)(2,1)} %param.27) | copy-start | bytes 3538948
  (64 other events, 505.7 us)
Sparse Core Ops, SparseCore 0:
  202.5 23.3 reduce-scatter.10
  305.9 21.4 reduce-scatter.12
  407.7 21.3 reduce-scatter.14
  442.2 62.8 reduce-scatter.24
  507.4 22.1 reduce-scatter.16
  533.7 62.5 reduce-scatter.22
  600.2 61.3 reduce-scatter.20
  665.8 61.4 reduce-scatter.18
where the time goes:
time: 744 us; the launch traced here: 735 us
  blocking collectives  306 us (41%)
  waiting for transfers between devices  224 us (30%)
  local copies, waits for them, and re-layouts  128 us (17%)
  matrix products  41.9 us (6%)
  between operations  15.8 us (2%)
  other arithmetic  14.1 us (2%)
    reduce_scatter x1, waiting for transfers between devices, shards(): lax.psum_scatter(grad_query_full, 'dp', scatter_dimension=0, tiled=True)  65.7 us
    reduce_scatter x1, waiting for transfers between devices, shards(): lax.psum_scatter(grad_key_full, 'dp', scatter_dimension=0, tiled=True)  65.3 us
    all_to_all x2, blocking collectives, send_experts(): lax.all_to_all(operand, 'dp', split_axis=0, concat_axis=0, tiled=True)  54.6 us
    reduce_scatter x4, waiting for transfers between devices, seq_scatter(): lax.psum_scatter(operand.astype(jnp.bfloat16), 'tensor', scatter_dimensio...  49.7 us
    psum x1, blocking collectives, shards(): lax.psum((gain_one_part, gain_two_part, bias_full, grad_router), ('dp', '...  40.5 us
    all_gather x4, blocking collectives, seq_gather(): return lax.all_gather(operand, 'tensor', axis=0, tiled=True)  33.1 us
    all_gather x1, blocking collectives, shards(): out_all = lax.all_gather(w_attn_out, 'dp', axis=1, tiled=True)  32.9 us
    all_gather x1, blocking collectives, shards(): lax.all_gather(w_value, 'dp', axis=0, tiled=True)  31.1 us
  transfers between devices with their start and end apart: 9, of which 7 were waited for; matrix products, arithmetic and copies ran while one was open for 12% of the time, Pallas kernels for 0%

commit v1 on v0

v1 whole, which is shorter than its diff:
```python
import jax
import jax.numpy as jnp
from jax import lax
from jax.experimental import pallas as pl
from jax.experimental.pallas import tpu as pltpu
from jax.sharding import PartitionSpec as P

DH = 64
EPS = 1e-06
NEG_FILL = -1e30
MESH = pl.DeviceIdType.MESH
VMEM_BYTES = 44 * 1024 * 1024


def round_up(count, unit):
    return (count + unit - 1) // unit * unit


def contract_rows(left, right):
    return lax.dot_general(
        left, right, (((0,), (0,)), ((), ())), preferred_element_type=jnp.float32
    )


def contract_cols(left, right):
    return lax.dot_general(
        left, right, (((1,), (1,)), ((), ())), preferred_element_type=jnp.float32
    )


def matmul(left, right):
    return jnp.dot(left, right, preferred_element_type=jnp.float32)


def norm_back(grad_norm, unit_rows, inv_rms, gain):
    scaled = grad_norm * gain
    return inv_rms * (scaled - unit_rows * jnp.mean(scaled * unit_rows, axis=-1, keepdims=True))


def greet(axes):
    barrier = pltpu.get_barrier_semaphore()
    total = 0
    for axis in axes:
        size = lax.axis_size(axis)
        me = lax.axis_index(axis)
        for shift in range(1, size):
            pl.semaphore_signal(
                barrier,
                inc=1,
                device_id={axis: lax.rem(me + shift, size)},
                device_id_type=MESH,
            )
        total += size - 1
    pl.semaphore_wait(barrier, total)


def push(source, target, sems, slot, axis, peer):
    copy = pltpu.make_async_remote_copy(
        src_ref=source,
        dst_ref=target,
        send_sem=sems.at[(0,) + slot],
        recv_sem=sems.at[(1,) + slot],
        device_id={axis: peer},
        device_id_type=MESH,
    )
    copy.start()
    return copy


def sibling_of(place):
    return place + 1 - 2 * lax.rem(place, 2)


class Swap:
    def __init__(self, axis):
        self.axis = axis

    def sems(self):
        return pltpu.SemaphoreType.DMA((2, lax.axis_size(self.axis)))

    def start(self, source, target, sems):
        size = lax.axis_size(self.axis)
        me = lax.axis_index(self.axis)
        self.copies = []
        for shift in range(1, size):
            peer = lax.rem(me + shift, size)
            self.copies.append(
                push(source.at[peer], target.at[me], sems, (shift,), self.axis, peer)
            )
        target[me] = source[me]

    def middle(self):
        pass

    def finish(self):
        for copy in self.copies:
            copy.wait()


class Gather:
    def __init__(self, axis):
        self.axis = axis

    def sems(self):
        return pltpu.SemaphoreType.DMA((2, 2, lax.axis_size(self.axis) // 2))

    def start(self, source, target, sems):
        size = lax.axis_size(self.axis)
        me = lax.axis_index(self.axis)
        self.target, self.s, self.size, self.me = target, sems, size, me
        self.copies = []
        for shift in range(1, size // 2):
            peer = lax.rem(me + 2 * shift, size)
            self.copies.append(push(source, target.at[me], sems, (0, shift), self.axis, peer))
        self.passed = [push(source, target.at[me], sems, (1, 0), self.axis, sibling_of(me))]
        target[me] = source[...]

    def middle(self):
        for shift in range(1, self.size // 2):
            self.copies[shift - 1].wait_recv()
            origin = lax.rem(self.me + self.size - 2 * shift, self.size)
            block = self.target.at[origin]
            self.passed.append(
                push(block, block, self.s, (1, shift), self.axis, sibling_of(self.me))
            )

    def finish(self):
        for copy in self.copies:
            copy.wait_send()
        for copy in self.passed:
            copy.wait()


def transfer(number, axes, moves, operands, shapes):
    count = len(moves)

    def kernel(*refs):
        sources, targets, sems = refs[:count], refs[count : 2 * count], refs[2 * count :]
        greet(axes)
        for move, source, target, sem in zip(moves, sources, targets, sems):
            move.start(source, target, sem)
        for move in moves:
            move.middle()
        for move in moves:
            move.finish()

    return pl.pallas_call(
        kernel,
        out_shape=[jax.ShapeDtypeStruct(s, o.dtype) for s, o in zip(shapes, operands)],
        in_specs=[pl.BlockSpec(memory_space=pltpu.VMEM)] * count,
        out_specs=[pl.BlockSpec(memory_space=pltpu.VMEM)] * count,
        scratch_shapes=[move.sems() for move in moves],
        compiler_params=pltpu.CompilerParams(
            collective_id=number, has_side_effects=True, vmem_limit_bytes=VMEM_BYTES
        ),
    )(*operands)


def swap_rows(number, operand):
    return transfer(number, ("tensor",), [Swap("tensor")], [operand], [operand.shape])[0]


def to_experts(number, operand):
    size, slots, columns = operand.shape
    ranks = lax.axis_size("tensor")

    def kernel(source, target, far, near):
        me, rank = lax.axis_index("dp"), lax.axis_index("tensor")
        across, beside = lax.rem(rank + 2, ranks), sibling_of(rank)
        greet(("dp", "tensor"))
        arrivals = [None]
        for shift in range(1, size):
            peer = lax.rem(me + shift, size)
            arrivals.append(push(source.at[peer], target.at[rank, me], far, (shift,), "dp", peer))
        target[rank, me] = source[me]
        first, second, third = [], [], []

        def relay(shift):
            first[shift].wait_recv()
            block = target.at[across, lax.rem(me + size - shift, size)]
            third.append(push(block, block, near, (2, shift), "tensor", beside))

        for shift in range(size):
            if shift > 0:
                arrivals[shift].wait_recv()
            block = target.at[rank, lax.rem(me + size - shift, size)]
            first.append(push(block, block, near, (0, shift), "tensor", across))
            second.append(push(block, block, near, (1, shift), "tensor", beside))
            if shift > 0:
                relay(shift - 1)
        relay(size - 1)
        for copy in arrivals[1:] + first:
            copy.wait_send()
        for copy in second + third:
            copy.wait()

    return pl.pallas_call(
        kernel,
        out_shape=jax.ShapeDtypeStruct((ranks, size, slots, columns), operand.dtype),
        in_specs=[pl.BlockSpec(memory_space=pltpu.VMEM)],
        out_specs=pl.BlockSpec(memory_space=pltpu.VMEM),
        scratch_shapes=[
            pltpu.SemaphoreType.DMA((2, size)),
            pltpu.SemaphoreType.DMA((2, 3, size)),
        ],
        compiler_params=pltpu.CompilerParams(
            collective_id=number, has_side_effects=True, vmem_limit_bytes=VMEM_BYTES
        ),
    )(operand)


def from_experts(number, operand):
    ranks, size, slots, columns = operand.shape

    def kernel(source, target, held, total, far, near):
        me, rank = lax.axis_index("dp"), lax.axis_index("tensor")
        greet(("dp", "tensor"))
        order = list(range(1, size)) + [0]
        pieces = {}
        for shift in order:
            group = lax.rem(me + shift, size)
            for step in range(1, ranks):
                peer = lax.rem(rank + step, ranks)
                pieces[shift, step] = push(
                    source.at[peer, group],
                    held.at[step, group],
                    near,
                    (step, shift),
                    "tensor",
                    peer,
                )
        sent = []
        for shift in order:
            group = lax.rem(me + shift, size)
            summed = source[rank, group].astype(jnp.float32)
            for step in range(1, ranks):
                pieces[shift, step].wait_recv()
                summed = summed + held[step, group].astype(jnp.float32)
            if shift == 0:
                target[me] = summed.astype(operand.dtype)
            else:
                total[group] = summed.astype(operand.dtype)
                sent.append(push(total.at[group], target.at[me], far, (shift,), "dp", group))
        for copy in pieces.values():
            copy.wait_send()
        for copy in sent:
            copy.wait()

    return pl.pallas_call(
        kernel,
        out_shape=jax.ShapeDtypeStruct((size, slots, columns), operand.dtype),
        in_specs=[pl.BlockSpec(memory_space=pltpu.VMEM)],
        out_specs=pl.BlockSpec(memory_space=pltpu.VMEM),
        scratch_shapes=[
            pltpu.VMEM((ranks, size, slots, columns), operand.dtype),
            pltpu.VMEM((size, slots, columns), operand.dtype),
            pltpu.SemaphoreType.DMA((2, size)),
            pltpu.SemaphoreType.DMA((2, ranks, size)),
        ],
        compiler_params=pltpu.CompilerParams(
            collective_id=number, has_side_effects=True, vmem_limit_bytes=VMEM_BYTES
        ),
    )(operand)


def last_sums(number, rows, weights, small):
    size, ranks = lax.axis_size("dp"), lax.axis_size("tensor")
    swap_t, swap_d = Swap("tensor"), Swap("dp")
    gather_t, gather_d = Gather("tensor"), Gather("dp")

    def kernel(rows_in, weights_in, small_in, rows_out, weights_out, small_out, held, total, *sems):
        greet(("dp", "tensor"))
        gather_t.start(small_in, held, sems[0])
        swap_d.start(weights_in, weights_out, sems[1])
        swap_t.start(rows_in, rows_out, sems[2])
        gather_t.middle()
        gather_t.finish()
        summed = held[0]
        for rank in range(1, ranks):
            summed = summed + held[rank]
        total[...] = summed
        gather_d.start(total, small_out, sems[3])
        swap_t.finish()
        swap_d.finish()
        gather_d.middle()
        gather_d.finish()

    return pl.pallas_call(
        kernel,
        out_shape=[
            jax.ShapeDtypeStruct(rows.shape, rows.dtype),
            jax.ShapeDtypeStruct(weights.shape, weights.dtype),
            jax.ShapeDtypeStruct((size,) + small.shape, small.dtype),
        ],
        in_specs=[pl.BlockSpec(memory_space=pltpu.VMEM)] * 3,
        out_specs=[pl.BlockSpec(memory_space=pltpu.VMEM)] * 3,
        scratch_shapes=[
            pltpu.VMEM((ranks,) + small.shape, small.dtype),
            pltpu.VMEM(small.shape, small.dtype),
            gather_t.sems(),
            swap_d.sems(),
            swap_t.sems(),
            gather_d.sems(),
        ],
        compiler_params=pltpu.CompilerParams(
            collective_id=number, has_side_effects=True, vmem_limit_bytes=VMEM_BYTES
        ),
    )(rows, weights, small)


def head_probs(queries, keys, line, seg_rows, seg_cols):
    tokens = queries.shape[0]
    spread = jnp.broadcast_to(line, (tokens, 2 * tokens))
    bias = pltpu.roll(spread, 0, 1, stride=1, stride_axis=0)[:, :tokens]
    raw = contract_cols(queries, keys) * DH ** (-0.5) + bias
    scores = jnp.where(seg_rows == seg_cols, raw, NEG_FILL)
    expo = jnp.exp(scores - jnp.max(scores, axis=-1, keepdims=True))
    return expo / jnp.sum(expo, axis=-1, keepdims=True)


def attend(qkv, lines, seg_rows, seg_cols):
    tokens, heads = qkv.shape[0], lines.shape[0]
    width = heads * DH

    def kernel(qkv_ref, lines_ref, rows_ref, cols_ref, out_ref):
        parts = []
        for head in range(heads):
            lo = head * DH
            queries = qkv_ref[:, lo : lo + DH]
            keys = qkv_ref[:, width + lo : width + lo + DH]
            values = qkv_ref[:, 2 * width + lo : 2 * width + lo + DH]
            probs = head_probs(
                queries, keys, lines_ref[head : head + 1, :], rows_ref[...], cols_ref[...]
            )
            parts.append(matmul(probs.astype(jnp.bfloat16), values).astype(jnp.bfloat16))
        out_ref[...] = jnp.concatenate(parts, axis=1)

    return pl.pallas_call(
        kernel,
        out_shape=jax.ShapeDtypeStruct((tokens, width), jnp.bfloat16),
        in_specs=[pl.BlockSpec(memory_space=pltpu.VMEM)] * 4,
        out_specs=pl.BlockSpec(memory_space=pltpu.VMEM),
        compiler_params=pltpu.CompilerParams(vmem_limit_bytes=VMEM_BYTES),
    )(qkv, lines, seg_rows, seg_cols)


def attend_back(qkv, lines, seg_rows, seg_cols, grad_heads):
    tokens, heads = qkv.shape[0], lines.shape[0]
    width = heads * DH

    def kernel(qkv_ref, lines_ref, rows_ref, cols_ref, grad_ref, out_ref, sums_ref):
        row = lax.broadcasted_iota(jnp.int32, (tokens, tokens), 0)
        col = lax.broadcasted_iota(jnp.int32, (tokens, tokens), 1)
        flip = (row + col == tokens - 1).astype(jnp.float32).astype(jnp.bfloat16)
        grads_q, grads_k, grads_v = [], [], []
        for head in range(heads):
            lo = head * DH
            queries = qkv_ref[:, lo : lo + DH]
            keys = qkv_ref[:, width + lo : width + lo + DH]
            values = qkv_ref[:, 2 * width + lo : 2 * width + lo + DH]
            grad = grad_ref[:, lo : lo + DH]
            probs = head_probs(
                queries, keys, lines_ref[head : head + 1, :], rows_ref[...], cols_ref[...]
            )
            grads_v.append(contract_rows(probs.astype(jnp.bfloat16), grad))
            grad_probs = contract_cols(grad, values)
            mean = jnp.sum(probs * grad_probs, axis=-1, keepdims=True)
            grad_scores = (probs * (grad_probs - mean)).astype(jnp.bfloat16)
            grads_q.append(matmul(grad_scores, keys) * DH ** (-0.5))
            grads_k.append(contract_rows(grad_scores, queries) * DH ** (-0.5))
            flipped = matmul(flip, grad_scores)
            padded = jnp.concatenate([flipped, jnp.zeros_like(flipped)], axis=1)
            lined = pltpu.roll(padded, 0, 1, stride=1, stride_axis=0)
            sums_ref[head : head + 1, :] = jnp.sum(lined, axis=0, keepdims=True)
        out_ref[...] = jnp.concatenate(grads_q + grads_k + grads_v, axis=1).astype(jnp.bfloat16)

    return pl.pallas_call(
        kernel,
        out_shape=[
            jax.ShapeDtypeStruct((tokens, 3 * width), jnp.bfloat16),
            jax.ShapeDtypeStruct((heads, 2 * tokens), jnp.float32),
        ],
        in_specs=[pl.BlockSpec(memory_space=pltpu.VMEM)] * 5,
        out_specs=[pl.BlockSpec(memory_space=pltpu.VMEM)] * 2,
        compiler_params=pltpu.CompilerParams(vmem_limit_bytes=VMEM_BYTES),
    )(qkv, lines, seg_rows, seg_cols, grad_heads)


def shards(
    layer_input,
    seq_lengths,
    expert_ids,
    bucket_table,
    gain_attn,
    gain_moe,
    w_query,
    w_key,
    w_value,
    w_attn_out,
    w_router,
    rel_bias,
    w_in,
    w_out,
    cotangent,
):
    float_type = jnp.float32
    half_type = jnp.bfloat16
    tok_dev, width = layer_input.shape
    group_tok = expert_ids.shape[0]
    experts = w_router.shape[1]
    groups, ranks = lax.axis_size("dp"), lax.axis_size("tensor")
    slots = round_up(group_tok // experts + 1, 16)
    local_heads = rel_bias.shape[1]
    head_cols = local_heads * DH
    max_length = (bucket_table.shape[0] + 1) // 2
    buckets = rel_bias.shape[0]
    row_dev = w_query.shape[0]
    row_pad = round_up(row_dev, 16)
    chunk = width // ranks
    tensor_rank = lax.axis_index("tensor")
    row_offset = tensor_rank * tok_dev

    places = jnp.arange(group_tok, dtype=jnp.int32)
    seq_lens = seq_lengths[0]
    seq_starts = jnp.cumsum(seq_lens) - seq_lens
    segment = jnp.sum((places[:, None] >= seq_starts[None, :]).astype(jnp.int32), axis=1) - 1
    seg_rows, seg_cols = segment[:, None], segment[None, :]
    line_bucket = jnp.concatenate(
        [
            bucket_table[max_length - 1 :],
            jnp.broadcast_to(bucket_table[-1:], (group_tok - max_length,)),
            jnp.broadcast_to(bucket_table[:1], (group_tok - max_length + 1,)),
            bucket_table[: max_length - 1],
        ]
    )
    line_hot = line_bucket[None, :] == jnp.arange(buckets, dtype=jnp.int32)[:, None]
    lines = contract_rows(rel_bias, line_hot.astype(half_type))

    input_f = layer_input.astype(float_type)
    gain_one = gain_attn.astype(float_type)
    inv_one = lax.rsqrt(jnp.mean(input_f * input_f, axis=-1, keepdims=True) + EPS)
    unit_one = input_f * inv_one
    normed_one = (unit_one * gain_one).astype(half_type)
    packed = jnp.concatenate([w_query, w_key, w_value, w_attn_out.T], axis=1)
    packed = jnp.pad(packed, ((0, row_pad - row_dev), (0, 0)))
    pack_cols = packed.shape[1]
    router_rows = round_up(experts, 16)
    router_cols = round_up(row_dev, 128)
    router_part = jnp.pad(
        w_router.T, ((0, router_rows - experts), (0, router_cols - row_dev))
    )
    packed_all, router_all, full_one = transfer(
        0,
        ("dp", "tensor"),
        [Gather("dp"), Gather("dp"), Gather("tensor")],
        [packed, router_part, normed_one],
        [
            (groups, row_pad, pack_cols),
            (groups, router_rows, router_cols),
            (ranks, tok_dev, width),
        ],
    )
    packed_all = packed_all[:, :row_dev].reshape(width, pack_cols)
    qkv_all, out_all = packed_all[:, : 3 * head_cols], packed_all[:, 3 * head_cols :]
    router_all = jnp.transpose(router_all[:, :experts, :row_dev], (1, 0, 2)).reshape(
        experts, width
    )
    full_one = full_one.reshape(group_tok, width)

    qkv = matmul(full_one, qkv_all).astype(half_type)
    head_out = attend(qkv, lines, seg_rows, seg_cols)
    attn_part = contract_cols(head_out, out_all).astype(half_type)
    attn_parts = swap_rows(1, attn_part.reshape(ranks, tok_dev, width))
    mixed = input_f + jnp.sum(attn_parts.astype(float_type), axis=0)

    gain_two = gain_moe.astype(float_type)
    inv_two = lax.rsqrt(jnp.mean(mixed * mixed, axis=-1, keepdims=True) + EPS)
    unit_two = mixed * inv_two
    normed_two = (unit_two * gain_two).astype(half_type)
    logits = contract_cols(normed_two, router_all)
    router_prob = jax.nn.softmax(logits, axis=-1)
    expert_row = expert_ids[:, 0]
    one_hot = (expert_row[:, None] == jnp.arange(experts, dtype=jnp.int32)[None, :]).astype(
        jnp.int32
    )
    earlier = (places[:, None] > places[None, :]).astype(half_type)
    before = matmul(earlier, one_hot.astype(half_type)).astype(jnp.int32)
    slot_index = jnp.sum(before * one_hot, axis=1)
    destination = expert_row * slots + slot_index
    place_hot = (
        destination[:, None] == jnp.arange(experts * slots, dtype=jnp.int32)[None, :]
    ).astype(half_type)
    own_choice = lax.dynamic_slice_in_dim(one_hot, row_offset, tok_dev, 0).astype(float_type)
    gate_prob = jnp.sum(router_prob * own_choice, axis=1, keepdims=True)
    grad_out = cotangent.astype(float_type)
    grad_y = (gate_prob * grad_out).astype(half_type)

    both = jnp.concatenate(
        [normed_two.reshape(tok_dev, ranks, chunk), grad_y.reshape(tok_dev, ranks, chunk)], axis=2
    )
    both = swap_rows(2, jnp.transpose(both, (1, 0, 2))).reshape(group_tok, 2 * chunk)
    buffer = contract_rows(place_hot, both).astype(half_type)
    arrived = to_experts(3, buffer.reshape(experts, slots, 2 * chunk))
    arrived = jnp.transpose(arrived.reshape(ranks, groups * slots, 2, chunk), (2, 1, 0, 3))
    arrived = arrived.reshape(2, groups * slots, width)
    rows, grad_rows_y = arrived[0], arrived[1]

    hidden = matmul(rows, w_in[0])
    activated = jax.nn.gelu(hidden, approximate=False).astype(half_type)
    partial_value = matmul(activated, w_out[0])
    grad_w_out = contract_rows(activated, grad_rows_y)
    grad_act = contract_cols(grad_rows_y, w_out[0])
    grad_hidden = jax.vjp(lambda operand: jax.nn.gelu(operand, approximate=False), hidden)[1](
        grad_act
    )[0].astype(half_type)
    grad_w_in = contract_rows(rows, grad_hidden)
    grad_rows = contract_cols(grad_hidden, w_in[0])

    back = jnp.concatenate(
        [
            partial_value.astype(half_type).reshape(groups * slots, ranks, chunk),
            grad_rows.astype(half_type).reshape(groups * slots, ranks, chunk),
        ],
        axis=2,
    )
    back = jnp.transpose(back, (1, 0, 2)).reshape(ranks, groups, slots, 2 * chunk)
    returned = from_experts(4, back).reshape(experts * slots, 2 * chunk)
    returned = matmul(place_hot, returned).astype(half_type)
    returned = swap_rows(5, returned.reshape(ranks, tok_dev, 2 * chunk))
    returned = jnp.transpose(returned.reshape(ranks, tok_dev, 2, chunk), (2, 1, 0, 3))
    returned = returned.reshape(2, tok_dev, width).astype(float_type)
    expert_y, grad_norm_two = returned[0], returned[1]
    layer_output = (mixed + gate_prob * expert_y).astype(half_type)
    grad_gate = jnp.sum(grad_out * expert_y, axis=1, keepdims=True)
    grad_logits = (router_prob * (own_choice - gate_prob) * grad_gate).astype(half_type)
    grad_router = contract_rows(grad_logits, normed_two)
    grad_norm_two = grad_norm_two + matmul(grad_logits, router_all)
    gain_two_part = jnp.sum(grad_norm_two * unit_two, axis=0)
    grad_mixed = grad_out + norm_back(grad_norm_two, unit_two, inv_two, gain_two)

    grad_attn = transfer(
        6,
        ("tensor",),
        [Gather("tensor")],
        [grad_mixed.astype(half_type)],
        [(ranks, tok_dev, width)],
    )[0].reshape(group_tok, width)
    grad_out_proj = contract_rows(grad_attn, head_out)
    grad_heads = matmul(grad_attn, out_all).astype(half_type)
    grad_qkv, line_sums = attend_back(qkv, lines, seg_rows, seg_cols, grad_heads)
    sums_hot = jnp.roll(line_hot, group_tok - 1, axis=1).astype(float_type)
    grad_bucket = lax.dot_general(
        line_sums, sums_hot, (((1,), (1,)), ((), ())), precision=lax.Precision.HIGHEST
    )
    grad_full_one = contract_cols(grad_qkv, qkv_all)
    gain_one_part = jnp.sum(grad_full_one * full_one.astype(float_type), axis=0) / gain_one
    grad_weights = jnp.concatenate(
        [contract_rows(full_one, grad_qkv), grad_out_proj], axis=1
    ).astype(half_type)
    grad_weights = jnp.pad(
        grad_weights.reshape(groups, row_dev, pack_cols),
        ((0, 0), (0, row_pad - row_dev), (0, 0)),
    )
    bias_flat = grad_bucket.reshape(1, local_heads * buckets)
    bias_row = jnp.pad(bias_flat, ((0, 0), (0, width - local_heads * buckets)))
    own_rank = (jnp.arange(ranks, dtype=jnp.int32) == tensor_rank).astype(float_type)
    small = jnp.concatenate(
        [gain_one_part[None], gain_two_part[None], own_rank[:, None] * bias_row, grad_router]
    )
    small = jnp.pad(small, ((0, round_up(small.shape[0], 8) - small.shape[0]), (0, 0)))
    norm_parts, weight_parts, small_parts = last_sums(
        7, grad_full_one.astype(half_type).reshape(ranks, tok_dev, width), grad_weights, small
    )
    grad_norm_one = jnp.sum(norm_parts.astype(float_type), axis=0)
    grad_input = grad_mixed + norm_back(grad_norm_one, unit_one, inv_one, gain_one)
    weight_sums = jnp.sum(weight_parts[:, :row_dev].astype(float_type), axis=0)
    small_sums = jnp.sum(small_parts, axis=0)
    router_sum = lax.dynamic_slice(
        small_sums, (2 + ranks, lax.axis_index("dp") * row_dev), (experts, row_dev)
    )
    bias_sum = lax.dynamic_slice_in_dim(small_sums, 2 + tensor_rank, 1, 0)
    bias_sum = bias_sum[0, : local_heads * buckets].reshape(local_heads, buckets)
    return (
        layer_output,
        grad_input,
        small_sums[0],
        small_sums[1],
        weight_sums[:, :head_cols],
        weight_sums[:, head_cols : 2 * head_cols],
        weight_sums[:, 2 * head_cols : 3 * head_cols],
        weight_sums[:, 3 * head_cols :].T,
        router_sum.T,
        bias_sum.T,
        grad_w_in[None],
        grad_w_out[None],
    )


def solution(mesh):
    return jax.shard_map(
        shards,
        mesh=mesh,
        in_specs=(
            P(("dp", "tensor"), None),
            P("dp", None),
            P("dp", None),
            P(),
            P(),
            P(),
            P("dp", "tensor"),
            P("dp", "tensor"),
            P("dp", "tensor"),
            P("tensor", "dp"),
            P("dp", None),
            P(None, "tensor"),
            P("dp", None, "tensor"),
            P("dp", "tensor", None),
            P(("dp", "tensor"), None),
        ),
        out_specs=(
            P(("dp", "tensor"), None),
            P(("dp", "tensor"), None),
            P(),
            P(),
            P("dp", "tensor"),
            P("dp", "tensor"),
            P("dp", "tensor"),
            P("tensor", "dp"),
            P("dp", None),
            P(None, "tensor"),
            P("dp", None, "tensor"),
            P("dp", "tensor", None),
        ),
        check_vma=False,
    )
```

time: 744 us -> 265 us (0.36); the launches traced: 735 us -> 263 us
  blocking collectives: 306 us -> 0 us
  waiting for transfers between devices: 224 us -> 0 us
  Pallas kernels: 0 us -> 160 us
  local copies, waits for them, and re-layouts: 128 us -> 49 us
  between operations: 15.8 us -> 1.51 us
    reduce_scatter x7 -> x0, waiting for transfers between devices: 202 us -> none  [the longest x1 65.7 us: shards(): lax.psum_scatter(grad_query_full, 'dp', scatter_dimension=0, tiled=True)]
    all_gather x9 -> x0, blocking collectives: 185 us -> none  [the longest x4 33.1 us: seq_gather(): return lax.all_gather(operand, 'tensor', axis=0, tiled=True)]
    pallas_call x0 -> x10, Pallas kernels: none -> 160 us  [the longest x5 57.1 us: transfer(): pl.pallas_call(kernel, out_shape=[jax.ShapeDtypeStruct(s, o.dtype) for s,...]
    all_to_all x3 -> x0, blocking collectives: 80.4 us -> none  [the longest x2 54.6 us: send_experts(): lax.all_to_all(operand, 'dp', split_axis=0, concat_axis=0, tiled=True)]
    psum x1 -> x0, blocking collectives: 40.5 us -> none  [shards(): lax.psum((gain_one_part, gain_two_part, bias_full, grad_router), ('dp', '...]
    reshape x8 -> x5, local copies, waits for them, and re-layouts: 28.1 us -> 3.62 us  [the longest x1 3.13 us: shards(): arrived.reshape(ranks, groups * slots, 2, chunk)]
    all_to_all x1 -> x0, waiting for transfers between devices: 21.9 us -> none  [return_rows(): lax.all_to_all(partial_value.reshape(groups, capacity, width).astype(jnp....]
    unnamed x181 -> x84, local copies, waits for them, and re-layouts: 25.8 us -> 7.34 us
  transfers between devices with their start and end apart: 9 -> 0, of which waited for: 7 -> 0; matrix products, arithmetic and copies ran while one was open for 12% -> 0% of each run, Pallas kernels for 0% -> 0%
where the time goes in v1:
time: 265 us; the launch traced here: 263 us
  Pallas kernels  160 us (60%)
  local copies, waits for them, and re-layouts  49 us (18%)
  matrix products  40 us (15%)
  other arithmetic  13 us (5%)
    pallas_call x5, Pallas kernels, transfer(): pl.pallas_call(kernel, out_shape=[jax.ShapeDtypeStruct(s, o.dtype) for s,...  57.1 us
    pallas_call x1, Pallas kernels, last_sums(): pl.pallas_call(kernel, out_shape=[jax.ShapeDtypeStruct(rows.shape, rows.d...  37.5 us
    pallas_call x1, Pallas kernels, from_experts(): pl.pallas_call(kernel, out_shape=jax.ShapeDtypeStruct((size, slots, colum...  29.4 us
    pallas_call x1, Pallas kernels, to_experts(): pl.pallas_call(kernel, out_shape=jax.ShapeDtypeStruct((ranks, size, slots...  25.9 us
    slice x3, local copies, waits for them, and re-layouts, shards(): rows, grad_rows_y = (arrived[0], arrived[1])  18.9 us
    dot_general x7, matrix products, matmul(): return jnp.dot(left, right, preferred_element_type=jnp.float32)  18.8 us
    dot_general x7, matrix products, contract_rows(): lax.dot_general(left, right, (((0,), (0,)), ((), ())), preferred_element_...  13.4 us
    dot_general x5, matrix products, contract_cols(): lax.dot_general(left, right, (((1,), (1,)), ((), ())), preferred_element_...  7.59 us

profile of v1, /device:TPU:0, one launch (start us, length us, event | category | flops | bytes accessed | tf_op | source)
XLA Modules:
  0.0 263.4 jit_solution(12269668201541092187)
XLA Ops:
  3.7 1.3 fusion.51
  16.5 25.1 %shard_map.238 = (bf16[8,96,768]{2,1,0:T(8,128)(2,1)S(1)}, bf16[8,16,128]{2,1,0:T(8,128)(2,1)S(1)}, bf16[4,128,768]{2,1,0:T(8,128)(2,1)S(1)}) custom-call(bf16[96,768]{1,0:T(8,128)(2,1)S(1)} %pad_maximum_fusion.1.refs_0_, bf16[16,128]{1,0:T(8,128)(2,1)S(1)} %pad.12.refs_1_, bf16[128,768]{1,0:T(8,128)(2,1)S(1)} %fusion.29.refs_2_), custom_call_target="tpu_custom_call" | custom-call | tf_op jit(solution)/shard_map/pallas_call | solution.py:147
  42.8 2.2 convolution_convert_fusion.4.qkv_ref
  45.0 4.1 %shard_map.239 = bf16[512,192]{1,0:T(8,128)(2,1)S(1)} custom-call(bf16[512,576]{1,0:T(8,128)(2,1)S(1)} %convolution_convert_fusion.4.qkv_ref, f32[3,1024]{1,0:T(4,128)S(1)} %convolution_bitcast_fusion.2.lines_ref, s32[512,1]{1,0:T(8,128)S(1)} %copy.118.rows_ref, s32[1,512]{1,0:T(1,128)S(1)} %bitcast.117), custom_call_target="tpu_custom_call" | custom-call | tf_op jit(solution)/shard_map/pallas_call | solution.py:338
  49.9 1.6 convolution_convert_fusion.3
  51.5 9.9 %shard_map.240 = bf16[4,128,768]{2,1,0:T(8,128)(2,1)S(1)} custom-call(bf16[4,128,768]{2,1,0:T(8,128)(2,1)S(1)} %bitcast.104), custom_call_target="tpu_custom_call" | custom-call | tf_op jit(solution)/shard_map/pallas_call | solution.py:147
  63.7 6.8 %shard_map.241 = bf16[4,128,384]{2,1,0:T(8,128)(2,1)S(1)} custom-call(bf16[4,128,384]{2,1,0:T(8,128)(2,1)S(1)} %maximum_bitcast_fusion.1.refs_0_), custom_call_target="tpu_custom_call" | custom-call | tf_op jit(solution)/shard_map/pallas_call | solution.py:147
  70.6 1.4 fusion.8
  74.2 25.9 %shard_map.242 = bf16[4,8,80,384]{3,2,1,0:T(8,128)(2,1)S(1)} custom-call(bf16[8,80,384]{2,1,0:T(8,128)(2,1)S(1)} %bitcast.112), custom_call_target="tpu_custom_call" | custom-call | tf_op jit(solution)/shard_map/pallas_call | solution.py:197
  100.1 3.1 %reshape.163 = bf16[4,640,2,192]{3,2,1,0:T(2,128)(2,1)} reshape(bf16[4,8,80,384]{3,2,1,0:T(8,128)(2,1)S(1)} %shard_map.242) | data formatting | bytes 3932160 | tf_op jit(solution)/shard_map/reshape | solution.py:504
  103.2 8.2 %fusion.49 = (bf16[1,640,4,192]{3,0,1,2:T(2,128)(2,1)}, bf16[1,640,4,192]{3,0,1,2:T(2,128)(2,1)}) fusion(bf16[2,640,4,192]{3,0,1,2:T(2,128)(2,1)} %bitcast.119), kind=kLoop, calls=%fused_computation.119 | loop fusion | bytes 3932160 | tf_op jit(solution)/shard_map/slice | solution.py:506
  111.4 5.2 %copy.126 = bf16[1,640,4,192]{1,3,2,0:T(8,128)(2,1)S(1)} copy(bf16[1,640,4,192]{3,0,1,2:T(2,128)(2,1)} %get-tuple-element.96) | data formatting | bytes 1966080 | tf_op jit(solution)/shard_map/slice | solution.py:506
  116.7 5.5 %copy.124 = bf16[1,640,4,192]{1,3,2,0:T(8,128)(2,1)S(1)} copy(bf16[1,640,4,192]{3,0,1,2:T(2,128)(2,1)} %get-tuple-element.97) | data formatting | bytes 1966080 | tf_op jit(solution)/shard_map/slice | solution.py:506
  122.2 11.2 %multiply_convert_fusion = (bf16[640,768]{1,0:T(8,128)(2,1)}, f32[640,768]{1,0:T(8,128)S(1)}, f32[640,768]{1,0:T(8,128)S(1)}) fusion(bf16[640,768]{0,1:T(8,128)(2,1)S(1)} %bitcast.128, bf16[1,768,768]{2,1,0:T(8,128)(2,1)S(1)} %copy-done), kind=kOutput, calls=%fused_computation.5 | convolution fusion | flops 786923520 | bytes 7077888 | tf_op jit(solution)/shard_map/dot_general | solution.py:32
  133.4 1.5 add_convert_fusion
  135.8 1.9 convolution_convert_fusion
  137.8 1.6 copy.127
  139.3 3.9 %convolution_bitcast_fusion.1 = f32[1,768,768]{2,1,0:T(8,128)} fusion(bf16[640,768]{0,1:T(8,128)(2,1)S(1)} %bitcast.129, bf16[640,768]{1,0:T(8,128)(2,1)} %copy-done.40), kind=kOutput, calls=%fused_computation.20 | convolution fusion | flops 754974720 | bytes 4325376 | tf_op jit(solution)/shard_map/dot_general | solution.py:20
  143.2 1.9 convolution_convert_fusion.1
  145.1 1.6 copy.125
  146.6 1.4 maximum_bitcast_fusion
  148.1 3.1 %copy.128 = bf16[4,640,384]{2,1,0:T(8,128)(2,1)S(1)} copy(bf16[4,640,384]{1,2,0:T(8,128)(2,1)} %maximum_bitcast_fusion) | data formatting | bytes 3932160 | tf_op jit(solution)/shard_map/transpose | solution.py:526
  151.2 29.4 %shard_map.243 = bf16[8,80,384]{2,1,0:T(8,128)(2,1)S(1)} custom-call(bf16[4,8,80,384]{3,2,1,0:T(8,128)(2,1)S(1)} %bitcast.101), custom_call_target="tpu_custom_call" | custom-call | tf_op jit(solution)/shard_map/pallas_call | solution.py:249
  181.1 5.9 %shard_map.244 = bf16[4,128,384]{2,1,0:T(8,128)(2,1)S(1)} custom-call(bf16[4,128,384]{2,1,0:T(8,128)(2,1)S(1)} %bitcast.114), custom_call_target="tpu_custom_call" | custom-call | tf_op jit(solution)/shard_map/pallas_call | solution.py:147
  191.1 2.5 convolution_bitcast_fusion
  193.7 9.4 %shard_map.245 = bf16[4,128,768]{2,1,0:T(8,128)(2,1)S(1)} custom-call(bf16[128,768]{1,0:T(8,128)(2,1)S(1)} %fusion.47.refs_0_), custom_call_target="tpu_custom_call" | custom-call | tf_op jit(solution)/shard_map/pallas_call | solution.py:147
  203.1 1.6 convolution_convert_fusion.6
  204.8 6.0 %shard_map.246 = (bf16[512,576]{1,0:T(8,128)(2,1)S(1)}, f32[3,1024]{1,0:T(4,128)S(1)}) custom-call(bf16[512,576]{1,0:T(8,128)(2,1)S(1)} %copy-done.2, f32[3,1024]{1,0:T(4,128)S(1)} %convolution_bitcast_fusion.2.lines_ref, s32[512,1]{1,0:T(8,128)S(1)} %copy.118.rows_ref, s32[1,512]{1,0:T(1,128)S(1)} %bitcast.118, bf16[512,192]{1,0:T(8,128)(2,1)S(1)} %copy.134.grad_ref), custom_call_target="tpu_custom_call" | custom-call | tf_op jit(solution)/shard_map/pallas_call | solution.py:377
  210.9 2.5 multiply_reduce_fusion
  214.5 3.1 %convolution_convert_fusion.2 = bf16[8,96,576]{2,1,0:T(8,128)(2,1)} fusion(bf16[8,96,512]{2,1,0:T(8,128)(2,1)} %bitcast.132, bf16[512,576]{1,0:T(8,128)(2,1)} %copy-done.9), kind=kOutput, calls=%fused_computation.26 | convolution fusion | flops 453427200 | bytes 2260992 | tf_op jit(solution)/shard_map/dot_general | solution.py:20
  218.8 1.6 convolution_convert_fusion.5
  220.8 37.5 %shard_map.247 = (bf16[4,128,768]{2,1,0:T(8,128)(2,1)S(1)}, bf16[8,96,768]{2,1,0:T(8,128)(2,1)S(1)}, f32[8,16,768]{2,1,0:T(8,128)S(1)}) custom-call(bf16[4,128,768]{2,1,0:T(8,128)(2,1)S(1)} %bitcast.107, bf16[8,96,768]{2,1,0:T(8,128)(2,1)S(1)} %pad_maximum_fusion.weights_in, f32[16,768]{1,0:T(8,128)S(1)} %copy-done.8), custom_call_target="tpu_custom_call" | custom-call | tf_op jit(solution)/shard_map/pallas_call | solution.py:288
  (159 shorter events, 34.2 us)
Async XLA Ops:
  0.6 121.5 %copy-start = (bf16[1,768,768]{2,1,0:T(8,128)(2,1)S(1)}, bf16[1,768,768]{2,1,0:T(8,128)(2,1)}, u32[]{:S(2)}) copy-start(bf16[1,768,768]{2,1,0:T(8,128)(2,1)} %param.27) | copy-start | bytes 3538948
  3.7 39.0 %copy-start.29 = (f32[128]{0:T(128)}, f32[128]{0:T(128)S(1)}, u32[]{:S(2)}) copy-start(f32[128]{0:T(128)S(1)} %add_rsqrt_fusion.1) | copy-start | bytes 1540
  8.2 62.4 %copy-start.33 = (s32[512,1]{0,1:T(1,128)}, s32[512,1]{0,1:T(1,128)S(1)}, u32[]{:S(2)}) copy-start(s32[512,1]{0,1:T(1,128)S(1)} %multiply_add_fusion) | copy-start | bytes 6148
  13.3 31.7 %copy-start.27 = (pred[32,1024]{1,0:T(32,128)(4,1)}, pred[32,1024]{1,0:T(32,128)(4,1)S(1)}, u32[]{:S(2)}) copy-start(pred[32,1024]{1,0:T(32,128)(4,1)S(1)} %iota_compare_fusion.9) | copy-start | bytes 98308
  42.7 29.3 %copy-start.5 = (bf16[4,128,768]{2,1,0:T(8,128)(2,1)}, bf16[4,128,768]{2,1,0:T(8,128)(2,1)S(1)}, u32[]{:S(2)}) copy-start(bf16[4,128,768]{2,1,0:T(8,128)(2,1)S(1)} %get-tuple-element.20) | copy-start | bytes 2359300
  49.9 11.6 %copy-start.3 = (bf16[512,192]{1,0:T(8,128)(2,1)}, bf16[512,192]{1,0:T(8,128)(2,1)S(1)}, u32[]{:S(2)}) copy-start(bf16[512,192]{1,0:T(8,128)(2,1)S(1)} %shard_map.239) | copy-start | bytes 589828
  49.9 11.6 %copy-start.13 = (bf16[128,768]{1,0:T(8,128)(2,1)S(1)}, bf16[128,768]{1,0:T(8,128)(2,1)}, u32[]{:S(2)}) copy-start(bf16[128,768]{1,0:T(8,128)(2,1)} %param.15) | copy-start | bytes 589828
  51.5 11.3 %copy-start.21 = (bf16[128,768]{1,0:T(8,128)(2,1)S(1)}, bf16[128,768]{1,0:T(8,128)(2,1)}, u32[]{:S(2)}) copy-start(bf16[128,768]{1,0:T(8,128)(2,1)} %param.29) | copy-start | bytes 589828
  62.5 8.0 %copy-start.19 = (bf16[128,768]{1,0:T(8,128)(2,1)}, bf16[128,768]{1,0:T(8,128)(2,1)S(1)}, u32[]{:S(2)}) copy-start(bf16[128,768]{1,0:T(8,128)(2,1)S(1)} %multiply_convert_fusion.1) | copy-start | bytes 589828
  116.7 16.7 %copy-start.24 = (bf16[1,640,4,192]{1,3,2,0:T(8,128)(2,1)}, bf16[1,640,4,192]{1,3,2,0:T(8,128)(2,1)S(1)}, u32[]{:S(2)}) copy-start(bf16[1,640,4,192]{1,3,2,0:T(8,128)(2,1)S(1)} %copy.126) | copy-start | bytes 2949124
  122.2 11.2 %copy-start.36 = (bf16[1,768,768]{2,1,0:T(8,128)(2,1)S(1)}, bf16[1,768,768]{2,1,0:T(8,128)(2,1)}, u32[]{:S(2)}) copy-start(bf16[1,768,768]{2,1,0:T(8,128)(2,1)} %param.28) | copy-start | bytes 3538948
  139.3 3.9 %copy-start.37 = (bf16[1,768,768]{2,1,0:T(8,128)(2,1)S(1)}, bf16[1,768,768]{2,1,0:T(8,128)(2,1)}, u32[]{:S(2)}) copy-start(bf16[1,768,768]{2,1,0:T(8,128)(2,1)} %param.28) | copy-start | bytes 3538948
  139.3 3.9 %copy-start.38 = (bf16[640,768]{1,0:T(8,128)(2,1)S(1)}, bf16[640,768]{1,0:T(8,128)(2,1)}, u32[]{:S(2)}) copy-start(bf16[640,768]{1,0:T(8,128)(2,1)} %get-tuple-element.92) | copy-start | bytes 2949124
  151.1 29.4 %copy-start.34 = (s32[512,1]{0,1:T(1,128)S(1)}, s32[512,1]{0,1:T(1,128)}, u32[]{:S(2)}) copy-start(s32[512,1]{0,1:T(1,128)} %copy-done.33) | copy-start | bytes 6148
  187.0 2.4 copy-start.22
  187.2 2.3 copy-start.20
  187.2 2.5 copy-start.11
  190.1 3.6 %copy-start.15 = (f32[128,768]{1,0:T(8,128)}, f32[128,768]{1,0:T(8,128)S(1)}, u32[]{:S(2)}) copy-start(f32[128,768]{1,0:T(8,128)S(1)} %get-tuple-element.113) | copy-start | bytes 1179652
  190.1 3.6 %copy-start.31 = (f32[128]{0:T(128)}, f32[128]{0:T(128)S(1)}, u32[]{:S(2)}) copy-start(f32[128]{0:T(128)S(1)} %broadcast_multiply_fusion.2) | copy-start | bytes 1540
  193.7 11.2 %copy-start.2 = (bf16[512,576]{1,0:T(8,128)(2,1)S(1)}, bf16[512,576]{1,0:T(8,128)(2,1)}, u32[]{:S(2)}) copy-start(bf16[512,576]{1,0:T(8,128)(2,1)} %copy-done.1) | copy-start | bytes 1769476
  210.8 2.6 copy-start.9
  210.9 2.6 slice-start
  210.9 2.8 %copy-start.28 = (bf16[768]{0:T(1024)(128)(2,1)S(1)}, bf16[768]{0:T(1024)(128)(2,1)}, u32[]{:S(2)}) copy-start(bf16[768]{0:T(1024)(128)(2,1)} %param.19) | copy-start | bytes 4612
  210.9 2.9 %copy-start.35 = (f32[4]{0:T(128)S(1)}, f32[4]{0:T(128)}, u32[]{:S(2)}) copy-start(f32[4]{0:T(128)} %compare_convert_fusion) | copy-start | bytes 52
  214.5 4.3 %copy-start.4 = (bf16[512,192]{1,0:T(8,128)(2,1)S(1)}, bf16[512,192]{1,0:T(8,128)(2,1)}, u32[]{:S(2)}) copy-start(bf16[512,192]{1,0:T(8,128)(2,1)} %copy-done.3) | copy-start | bytes 589828
  220.7 37.7 %copy-start.14 = (bf16[128,768]{1,0:T(8,128)(2,1)S(1)}, bf16[128,768]{1,0:T(8,128)(2,1)}, u32[]{:S(2)}) copy-start(bf16[128,768]{1,0:T(8,128)(2,1)} %param.15) | copy-start | bytes 589828
  220.7 37.7 %copy-start.30 = (f32[128]{0:T(128)S(1)}, f32[128]{0:T(128)}, u32[]{:S(2)}) copy-start(f32[128]{0:T(128)} %copy-done.29) | copy-start | bytes 1540
  220.7 37.9 %copy-start.12 = (f32[128,768]{1,0:T(8,128)S(1)}, f32[128,768]{1,0:T(8,128)}, u32[]{:S(2)}) copy-start(f32[128,768]{1,0:T(8,128)} %copy-done.10) | copy-start | bytes 1179652
  220.7 37.9 %copy-start.16 = (f32[128,768]{1,0:T(8,128)S(1)}, f32[128,768]{1,0:T(8,128)}, u32[]{:S(2)}) copy-start(f32[128,768]{1,0:T(8,128)} %copy-done.15) | copy-start | bytes 1179652
  220.7 37.9 %copy-start.18 = (f32[128,768]{1,0:T(8,128)S(1)}, f32[128,768]{1,0:T(8,128)}, u32[]{:S(2)}) copy-start(f32[128,768]{1,0:T(8,128)} %copy-done.17) | copy-start | bytes 1179652
  220.7 37.9 %copy-start.23 = (bf16[128,768]{1,0:T(8,128)(2,1)S(1)}, bf16[128,768]{1,0:T(8,128)(2,1)}, u32[]{:S(2)}) copy-start(bf16[128,768]{1,0:T(8,128)(2,1)} %param.29) | copy-start | bytes 589828
  220.7 37.9 %copy-start.32 = (f32[128]{0:T(128)S(1)}, f32[128]{0:T(128)}, u32[]{:S(2)}) copy-start(f32[128]{0:T(128)} %copy-done.31) | copy-start | bytes 1540
  (10 other events, 12.1 us)

commit v2 on v1

--- a/solution.py
+++ b/solution.py
@@ -131,6 +131,77 @@
             copy.wait()
 
 
+class Reduce:
+    def __init__(self, axis, shape, dtype):
+        self.axis = axis
+        self.half = lax.axis_size(axis) // 2
+        self.block, self.dtype = tuple(shape), dtype
+
+    def scratch(self):
+        slots = pltpu.VMEM((3, self.half) + self.block, self.dtype)
+        return [slots, pltpu.SemaphoreType.DMA((2, 2, self.half))]
+
+    def start(self, source, slots, sems):
+        self.source, self.slots, self.s = source, slots, sems
+        self.size, self.me = lax.axis_size(self.axis), lax.axis_index(self.axis)
+        sibling = sibling_of(self.me)
+        self.near = {}
+        for shift in list(range(1, self.half)) + [0]:
+            block = source.at[lax.rem(sibling + 2 * shift, self.size)]
+            self.near[shift] = push(
+                block, slots.at[0, shift], sems, (0, shift), self.axis, sibling
+            )
+
+    def middle(self):
+        self.far = {}
+        for shift in range(1, self.half):
+            self.near[shift].wait_recv()
+            peer = lax.rem(self.me + 2 * shift, self.size)
+            pair = self.source[peer].astype(jnp.float32)
+            pair = pair + self.slots[0, shift].astype(jnp.float32)
+            self.slots[1, shift] = pair.astype(self.dtype)
+            self.far[shift] = push(
+                self.slots.at[1, shift],
+                self.slots.at[2, shift],
+                self.s,
+                (1, shift),
+                self.axis,
+                peer,
+            )
+
+    def finish(self, target):
+        self.near[0].wait_recv()
+        summed = self.source[self.me].astype(jnp.float32)
+        summed = summed + self.slots[0, 0].astype(jnp.float32)
+        for shift in range(1, self.half):
+            self.far[shift].wait_recv()
+            summed = summed + self.slots[2, shift].astype(jnp.float32)
+        target[...] = summed
+        for copy in list(self.near.values()) + list(self.far.values()):
+            copy.wait_send()
+
+
+def sum_rows(number, operand):
+    move = Reduce("tensor", operand.shape[1:], operand.dtype)
+
+    def kernel(source, target, slots, sems):
+        greet(("tensor",))
+        move.start(source, slots, sems)
+        move.middle()
+        move.finish(target)
+
+    return pl.pallas_call(
+        kernel,
+        out_shape=jax.ShapeDtypeStruct(operand.shape[1:], jnp.float32),
+        in_specs=[pl.BlockSpec(memory_space=pltpu.VMEM)],
+        out_specs=pl.BlockSpec(memory_space=pltpu.VMEM),
+        scratch_shapes=move.scratch(),
+        compiler_params=pltpu.CompilerParams(
+            collective_id=number, has_side_effects=True, vmem_limit_bytes=VMEM_BYTES
+        ),
+    )(operand)
+
+
 def transfer(number, axes, moves, operands, shapes):
     count = len(moves)
 
@@ -160,136 +231,202 @@
     return transfer(number, ("tensor",), [Swap("tensor")], [operand], [operand.shape])[0]
 
 
-def to_experts(number, operand):
+def visit_experts(number, operand, weight_in, weight_out):
     size, slots, columns = operand.shape
     ranks = lax.axis_size("tensor")
-
-    def kernel(source, target, far, near):
+    chunk = columns // 2
+    width, units = weight_in.shape
+    half_type, float_type = jnp.bfloat16, jnp.float32
+    steps = min(4, size)
+    share = size // steps
+    step_rows = share * slots
+
+    def kernel(
+        source, w_in, w_out, target, grad_in, grad_out,
+        arrived, back, held, pairs, got, total, rows, grads, acts, hids, far, near, home, ret,
+    ):
         me, rank = lax.axis_index("dp"), lax.axis_index("tensor")
         across, beside = lax.rem(rank + 2, ranks), sibling_of(rank)
+        aslant = lax.rem(beside + 2, ranks)
+        groups = [lax.rem(me + size - shift, size) for shift in range(size)]
         greet(("dp", "tensor"))
         arrivals = [None]
         for shift in range(1, size):
             peer = lax.rem(me + shift, size)
-            arrivals.append(push(source.at[peer], target.at[rank, me], far, (shift,), "dp", peer))
-        target[rank, me] = source[me]
-        first, second, third = [], [], []
-
-        def relay(shift):
-            first[shift].wait_recv()
-            block = target.at[across, lax.rem(me + size - shift, size)]
-            third.append(push(block, block, near, (2, shift), "tensor", beside))
-
-        for shift in range(size):
-            if shift > 0:
-                arrivals[shift].wait_recv()
-            block = target.at[rank, lax.rem(me + size - shift, size)]
-            first.append(push(block, block, near, (0, shift), "tensor", across))
-            second.append(push(block, block, near, (1, shift), "tensor", beside))
-            if shift > 0:
-                relay(shift - 1)
-        relay(size - 1)
-        for copy in arrivals[1:] + first:
+            arrivals.append(push(source.at[peer], arrived.at[rank, me], far, (shift,), "dp", peer))
+        arrived[rank, me] = source[me]
+        first, second, third = {}, {}, {}
+        kept, passed, crossed, sent = {}, {}, {}, {}
+
+        def spread(step):
+            for shift in range(step * share, (step + 1) * share):
+                if shift > 0:
+                    arrivals[shift].wait_recv()
+                block = arrived.at[rank, groups[shift]]
+                first[shift] = push(block, block, near, (0, shift), "tensor", across)
+                second[shift] = push(block, block, near, (1, shift), "tensor", beside)
+
+        def relay(step):
+            for shift in range(step * share, (step + 1) * share):
+                first[shift].wait_recv()
+                block = arrived.at[across, groups[shift]]
+                third[shift] = push(block, block, near, (2, shift), "tensor", beside)
+
+        def compute(step):
+            lo = step * step_rows
+            for place in range(share):
+                shift = step * share + place
+                second[shift].wait_recv()
+                third[shift].wait_recv()
+                blocks = [arrived[place_t, groups[shift]] for place_t in range(ranks)]
+                at = slice(lo + place * slots, lo + (place + 1) * slots)
+                rows[at, :] = jnp.concatenate([block[:, :chunk] for block in blocks], axis=1)
+                grads[at, :] = jnp.concatenate([block[:, chunk:] for block in blocks], axis=1)
+            part = slice(lo, lo + step_rows)
+            hidden = matmul(rows[part, :], w_in[...])
+            below = 0.5 + 0.5 * lax.erf(hidden * (0.5**0.5))
+            slope = below + hidden * jnp.exp(-0.5 * hidden * hidden) * 0.3989422804014327
+            activated = (hidden * below).astype(half_type)
+            acts[part, :] = activated
+            grad_act = contract_cols(grads[part, :], w_out[...])
+            grad_hidden = (grad_act * slope).astype(half_type)
+            hids[part, :] = grad_hidden
+            value = matmul(activated, w_out[...]).astype(half_type)
+            grad_rows = contract_cols(grad_hidden, w_in[...]).astype(half_type)
+            for place in range(share):
+                shift = step * share + place
+                at = slice(place * slots, (place + 1) * slots)
+                for place_t in range(ranks):
+                    cols = slice(place_t * chunk, (place_t + 1) * chunk)
+                    back[place_t, groups[shift]] = jnp.concatenate(
+                        [value[at, cols], grad_rows[at, cols]], axis=1
+                    )
+
+        def pair_up(step):
+            for shift in range(step * share, (step + 1) * share):
+                group = groups[shift]
+                passed[shift] = push(
+                    back.at[aslant, group], held.at[1, group], home, (1, shift), "tensor", beside
+                )
+                kept[shift] = push(
+                    back.at[beside, group], held.at[0, group], home, (0, shift), "tensor", beside
+                )
+
+        def cross(step):
+            for shift in range(step * share, (step + 1) * share):
+                group = groups[shift]
+                passed[shift].wait_recv()
+                pair = back[across, group].astype(float_type) + held[1, group].astype(float_type)
+                pairs[group] = pair.astype(half_type)
+                crossed[shift] = push(
+                    pairs.at[group], got.at[group], home, (2, shift), "tensor", across
+                )
+
+        def send_home(step):
+            for shift in range(step * share, (step + 1) * share):
+                group = groups[shift]
+                kept[shift].wait_recv()
+                crossed[shift].wait_recv()
+                summed = back[rank, group].astype(float_type) + held[0, group].astype(float_type)
+                summed = (summed + got[group].astype(float_type)).astype(half_type)
+                if shift == 0:
+                    target[me] = summed
+                else:
+                    total[group] = summed
+                    sent[shift] = push(
+                        total.at[group], target.at[me], ret, (shift,), "dp", group
+                    )
+
+        spread(0)
+        for step in range(steps):
+            relay(step)
+            if step + 1 < steps:
+                spread(step + 1)
+            compute(step)
+            pair_up(step)
+            if step >= 1:
+                cross(step - 1)
+            if step >= 2:
+                send_home(step - 2)
+        if steps >= 2:
+            send_home(steps - 2)
+        cross(steps - 1)
+        grad_out[...] = contract_rows(acts[...], grads[...])
+        send_home(steps - 1)
+        grad_in[...] = contract_rows(rows[...], hids[...])
+        for copy in arrivals[1:]:
             copy.wait_send()
-        for copy in second + third:
+        for copies in (first, second, third, kept, passed, crossed):
+            for copy in copies.values():
+                copy.wait_send()
+        for copy in sent.values():
             copy.wait()
 
+    blocks = (size, slots, columns)
     return pl.pallas_call(
         kernel,
-        out_shape=jax.ShapeDtypeStruct((ranks, size, slots, columns), operand.dtype),
-        in_specs=[pl.BlockSpec(memory_space=pltpu.VMEM)],
-        out_specs=pl.BlockSpec(memory_space=pltpu.VMEM),
+        out_shape=[
+            jax.ShapeDtypeStruct(blocks, operand.dtype),
+            jax.ShapeDtypeStruct(weight_in.shape, float_type),
+            jax.ShapeDtypeStruct(weight_out.shape, float_type),
+        ],
+        in_specs=[pl.BlockSpec(memory_space=pltpu.VMEM)] * 3,
+        out_specs=[pl.BlockSpec(memory_space=pltpu.VMEM)] * 3,
         scratch_shapes=[
+            pltpu.VMEM((ranks,) + blocks, half_type),
+            pltpu.VMEM((ranks,) + blocks, half_type),
+            pltpu.VMEM((2,) + blocks, half_type),
+            pltpu.VMEM(blocks, half_type),
+            pltpu.VMEM(blocks, half_type),
+            pltpu.VMEM(blocks, half_type),
+            pltpu.VMEM((size * slots, width), half_type),
+            pltpu.VMEM((size * slots, width), half_type),
+            pltpu.VMEM((size * slots, units), half_type),
+            pltpu.VMEM((size * slots, units), half_type),
             pltpu.SemaphoreType.DMA((2, size)),
             pltpu.SemaphoreType.DMA((2, 3, size)),
+            pltpu.SemaphoreType.DMA((2, 3, size)),
+            pltpu.SemaphoreType.DMA((2, size)),
         ],
         compiler_params=pltpu.CompilerParams(
             collective_id=number, has_side_effects=True, vmem_limit_bytes=VMEM_BYTES
         ),
-    )(operand)
-
-
-def from_experts(number, operand):
-    ranks, size, slots, columns = operand.shape
-
-    def kernel(source, target, held, total, far, near):
-        me, rank = lax.axis_index("dp"), lax.axis_index("tensor")
-        greet(("dp", "tensor"))
-        order = list(range(1, size)) + [0]
-        pieces = {}
-        for shift in order:
-            group = lax.rem(me + shift, size)
-            for step in range(1, ranks):
-                peer = lax.rem(rank + step, ranks)
-                pieces[shift, step] = push(
-                    source.at[peer, group],
-                    held.at[step, group],
-                    near,
-                    (step, shift),
-                    "tensor",
-                    peer,
-                )
-        sent = []
-        for shift in order:
-            group = lax.rem(me + shift, size)
-            summed = source[rank, group].astype(jnp.float32)
-            for step in range(1, ranks):
-                pieces[shift, step].wait_recv()
-                summed = summed + held[step, group].astype(jnp.float32)
-            if shift == 0:
-                target[me] = summed.astype(operand.dtype)
-            else:
-                total[group] = summed.astype(operand.dtype)
-                sent.append(push(total.at[group], target.at[me], far, (shift,), "dp", group))
-        for copy in pieces.values():
-            copy.wait_send()
-        for copy in sent:
-            copy.wait()
-
-    return pl.pallas_call(
-        kernel,
-        out_shape=jax.ShapeDtypeStruct((size, slots, columns), operand.dtype),
-        in_specs=[pl.BlockSpec(memory_space=pltpu.VMEM)],
-        out_specs=pl.BlockSpec(memory_space=pltpu.VMEM),
-        scratch_shapes=[
-            pltpu.VMEM((ranks, size, slots, columns), operand.dtype),
-            pltpu.VMEM((size, slots, columns), operand.dtype),
-            pltpu.SemaphoreType.DMA((2, size)),
-            pltpu.SemaphoreType.DMA((2, ranks, size)),
-        ],
-        compiler_params=pltpu.CompilerParams(
-            collective_id=number, has_side_effects=True, vmem_limit_bytes=VMEM_BYTES
-        ),
-    )(operand)
+    )(operand, weight_in, weight_out)
 
 
 def last_sums(number, rows, weights, small):
     size, ranks = lax.axis_size("dp"), lax.axis_size("tensor")
-    swap_t, swap_d = Swap("tensor"), Swap("dp")
+    sum_t = Reduce("tensor", rows.shape[1:], rows.dtype)
+    sum_d = Reduce("dp", weights.shape[1:], weights.dtype)
     gather_t, gather_d = Gather("tensor"), Gather("dp")
 
-    def kernel(rows_in, weights_in, small_in, rows_out, weights_out, small_out, held, total, *sems):
+    def kernel(
+        rows_in, weights_in, small_in, rows_out, weights_out, small_out,
+        held, total, slots_t, sems_t, slots_d, sems_d, sems_g, sems_h,
+    ):
         greet(("dp", "tensor"))
-        gather_t.start(small_in, held, sems[0])
-        swap_d.start(weights_in, weights_out, sems[1])
-        swap_t.start(rows_in, rows_out, sems[2])
+        sum_d.start(weights_in, slots_d, sems_d)
+        gather_t.start(small_in, held, sems_g)
+        sum_t.start(rows_in, slots_t, sems_t)
         gather_t.middle()
+        sum_t.middle()
+        sum_d.middle()
         gather_t.finish()
         summed = held[0]
         for rank in range(1, ranks):
             summed = summed + held[rank]
         total[...] = summed
-        gather_d.start(total, small_out, sems[3])
-        swap_t.finish()
-        swap_d.finish()
+        gather_d.start(total, small_out, sems_h)
+        sum_t.finish(rows_out)
         gather_d.middle()
+        sum_d.finish(weights_out)
         gather_d.finish()
 
     return pl.pallas_call(
         kernel,
         out_shape=[
-            jax.ShapeDtypeStruct(rows.shape, rows.dtype),
-            jax.ShapeDtypeStruct(weights.shape, weights.dtype),
+            jax.ShapeDtypeStruct(rows.shape[1:], jnp.float32),
+            jax.ShapeDtypeStruct(weights.shape[1:], jnp.float32),
             jax.ShapeDtypeStruct((size,) + small.shape, small.dtype),
         ],
         in_specs=[pl.BlockSpec(memory_space=pltpu.VMEM)] * 3,
@@ -297,11 +434,10 @@
         scratch_shapes=[
             pltpu.VMEM((ranks,) + small.shape, small.dtype),
             pltpu.VMEM(small.shape, small.dtype),
-            gather_t.sems(),
-            swap_d.sems(),
-            swap_t.sems(),
-            gather_d.sems(),
-        ],
+        ]
+        + sum_t.scratch()
+        + sum_d.scratch()
+        + [gather_t.sems(), gather_d.sems()],
         compiler_params=pltpu.CompilerParams(
             collective_id=number, has_side_effects=True, vmem_limit_bytes=VMEM_BYTES
         ),
@@ -421,9 +557,11 @@
     row_offset = tensor_rank * tok_dev
 
     places = jnp.arange(group_tok, dtype=jnp.int32)
-    seq_lens = seq_lengths[0]
-    seq_starts = jnp.cumsum(seq_lens) - seq_lens
-    segment = jnp.sum((places[:, None] >= seq_starts[None, :]).astype(jnp.int32), axis=1) - 1
+    segment = jnp.zeros_like(places)
+    start = jnp.zeros((), jnp.int32)
+    for sequence in range(seq_lengths.shape[1] - 1):
+        start = start + seq_lengths[0, sequence]
+        segment = segment + (places >= start).astype(jnp.int32)
     seg_rows, seg_cols = segment[:, None], segment[None, :]
     line_bucket = jnp.concatenate(
         [
@@ -470,8 +608,7 @@
     qkv = matmul(full_one, qkv_all).astype(half_type)
     head_out = attend(qkv, lines, seg_rows, seg_cols)
     attn_part = contract_cols(head_out, out_all).astype(half_type)
-    attn_parts = swap_rows(1, attn_part.reshape(ranks, tok_dev, width))
-    mixed = input_f + jnp.sum(attn_parts.astype(float_type), axis=0)
+    mixed = input_f + sum_rows(1, attn_part.reshape(ranks, tok_dev, width))
 
     gain_two = gain_moe.astype(float_type)
     inv_two = lax.rsqrt(jnp.mean(mixed * mixed, axis=-1, keepdims=True) + EPS)
@@ -500,31 +637,11 @@
     )
     both = swap_rows(2, jnp.transpose(both, (1, 0, 2))).reshape(group_tok, 2 * chunk)
     buffer = contract_rows(place_hot, both).astype(half_type)
-    arrived = to_experts(3, buffer.reshape(experts, slots, 2 * chunk))
-    arrived = jnp.transpose(arrived.reshape(ranks, groups * slots, 2, chunk), (2, 1, 0, 3))
-    arrived = arrived.reshape(2, groups * slots, width)
-    rows, grad_rows_y = arrived[0], arrived[1]
-
-    hidden = matmul(rows, w_in[0])
-    activated = jax.nn.gelu(hidden, approximate=False).astype(half_type)
-    partial_value = matmul(activated, w_out[0])
-    grad_w_out = contract_rows(activated, grad_rows_y)
-    grad_act = contract_cols(grad_rows_y, w_out[0])
-    grad_hidden = jax.vjp(lambda operand: jax.nn.gelu(operand, approximate=False), hidden)[1](
-        grad_act
-    )[0].astype(half_type)
-    grad_w_in = contract_rows(rows, grad_hidden)
-    grad_rows = contract_cols(grad_hidden, w_in[0])
-
-    back = jnp.concatenate(
-        [
-            partial_value.astype(half_type).reshape(groups * slots, ranks, chunk),
-            grad_rows.astype(half_type).reshape(groups * slots, ranks, chunk),
-        ],
-        axis=2,
-    )
-    back = jnp.transpose(back, (1, 0, 2)).reshape(ranks, groups, slots, 2 * chunk)
-    returned = from_experts(4, back).reshape(experts * slots, 2 * chunk)
+    returned, grad_w_in, grad_w_out = visit_experts(
+        3, buffer.reshape(experts, slots, 2 * chunk), w_in[0], w_out[0]
+    )
+
+    returned = returned.reshape(experts * slots, 2 * chunk)
     returned = matmul(place_hot, returned).astype(half_type)
     returned = swap_rows(5, returned.reshape(ranks, tok_dev, 2 * chunk))
     returned = jnp.transpose(returned.reshape(ranks, tok_dev, 2, chunk), (2, 1, 0, 3))
@@ -568,12 +685,11 @@
         [gain_one_part[None], gain_two_part[None], own_rank[:, None] * bias_row, grad_router]
     )
     small = jnp.pad(small, ((0, round_up(small.shape[0], 8) - small.shape[0]), (0, 0)))
-    norm_parts, weight_parts, small_parts = last_sums(
+    grad_norm_one, weight_sums, small_parts = last_sums(
         7, grad_full_one.astype(half_type).reshape(ranks, tok_dev, width), grad_weights, small
     )
-    grad_norm_one = jnp.sum(norm_parts.astype(float_type), axis=0)
     grad_input = grad_mixed + norm_back(grad_norm_one, unit_one, inv_one, gain_one)
-    weight_sums = jnp.sum(weight_parts[:, :row_dev].astype(float_type), axis=0)
+    weight_sums = weight_sums[:row_dev]
     small_sums = jnp.sum(small_parts, axis=0)
     router_sum = lax.dynamic_slice(
         small_sums, (2 + ranks, lax.axis_index("dp") * row_dev), (experts, row_dev)

time: 265 us -> 192 us (0.72)
  matrix products: 40 us -> 11.8 us
  local copies, waits for them, and re-layouts: 49 us -> 26.5 us
  Pallas kernels: 160 us -> 141 us
  other arithmetic: 13 us -> 8.69 us
    slice x3 -> x1, local copies, waits for them, and re-layouts: 18.9 us -> 0.58 us  [shards(): start = start + seq_lengths[0, sequence]]
    dot_general x7 -> x5, matrix products: 18.8 us -> 4.56 us  [matmul(): return jnp.dot(left, right, preferred_element_type=jnp.float32)]
    pallas_call x5 -> x4, Pallas kernels: 57.1 us -> 45.9 us  [transfer(): pl.pallas_call(kernel, out_shape=[jax.ShapeDtypeStruct(s, o.dtype) for s,...]
    dot_general x7 -> x5, matrix products: 13.4 us -> 4.14 us  [contract_rows(): lax.dot_general(left, right, (((0,), (0,)), ((), ())), preferred_element_...]
    pallas_call x3, Pallas kernels: 92.8 us -> 85.2 us  [the longest x1 46.7 us: visit_experts(): pl.pallas_call(kernel, out_shape=[jax.ShapeDtypeStruct(blocks, operand.dt...]
    dot_general x5 -> x3, matrix products: 7.59 us -> 2.89 us  [contract_cols(): lax.dot_general(left, right, (((1,), (1,)), ((), ())), preferred_element_...]
    unnamed x84 -> x68, local copies, waits for them, and re-layouts: 7.34 us -> 11 us
    reshape x1 -> x0, local copies, waits for them, and re-layouts: 3.13 us -> none  [shards(): arrived.reshape(ranks, groups * slots, 2, chunk)]
where the time goes in v2:
time: 192 us; the launch traced here: 191 us
  Pallas kernels  141 us (73%)
  local copies, waits for them, and re-layouts  26.5 us (14%)
  matrix products  11.8 us (6%)
  other arithmetic  8.69 us (5%)
  between operations  2.73 us (1%)
    pallas_call x1, Pallas kernels, visit_experts(): pl.pallas_call(kernel, out_shape=[jax.ShapeDtypeStruct(blocks, operand.dt...  46.7 us
    pallas_call x4, Pallas kernels, transfer(): pl.pallas_call(kernel, out_shape=[jax.ShapeDtypeStruct(s, o.dtype) for s,...  45.9 us
    pallas_call x1, Pallas kernels, last_sums(): pl.pallas_call(kernel, out_shape=[jax.ShapeDtypeStruct(rows.shape[1:], jn...  29.8 us
    unnamed x68, local copies, waits for them, and re-layouts  11 us
    pallas_call x1, Pallas kernels, sum_rows(): pl.pallas_call(kernel, out_shape=jax.ShapeDtypeStruct(operand.shape[1:],...  8.74 us
    pallas_call x1, Pallas kernels, attend_back(): pl.pallas_call(kernel, out_shape=[jax.ShapeDtypeStruct((tokens, 3 * width...  6.02 us
    dot_general x5, matrix products, matmul(): return jnp.dot(left, right, preferred_element_type=jnp.float32)  4.56 us
    dot_general x5, matrix products, contract_rows(): lax.dot_general(left, right, (((0,), (0,)), ((), ())), preferred_element_...  4.14 us

profile of v2, /device:TPU:0, one launch (start us, length us, event | category | flops | bytes accessed | tf_op | source)
XLA Modules:
  0.0 190.9 jit_solution(18233500641703518921)
XLA Ops:
  1.3 1.0 fusion.20
  2.9 1.0 fusion.15.refs_2_
  4.0 0.9 copy.55
  4.9 1.0 pad_maximum_fusion.1.refs_0_
  6.5 25.0 %shard_map.238 = (bf16[8,96,768]{2,1,0:T(8,128)(2,1)S(1)}, bf16[8,16,128]{2,1,0:T(8,128)(2,1)S(1)}, bf16[4,128,768]{2,1,0:T(8,128)(2,1)S(1)}) custom-call(bf16[96,768]{1,0:T(8,128)(2,1)S(1)} %pad_maximum_fusion.1.refs_0_, bf16[16,128]{1,0:T(8,128)(2,1)S(1)} %pad.12.refs_1_, bf16[128,768]{1,0:T(8,128)(2,1)S(1)} %fusion.15.refs_2_), custom_call_target="tpu_custom_call" | custom-call | tf_op jit(solution)/shard_map/pallas_call | solution.py:218
  31.5 0.8 convolution_convert_fusion.2.qkv_ref
  37.8 4.1 %shard_map.239 = bf16[512,192]{1,0:T(8,128)(2,1)S(1)} custom-call(bf16[512,576]{1,0:T(8,128)(2,1)S(1)} %convolution_convert_fusion.2.qkv_ref, f32[3,1024]{1,0:T(4,128)S(1)} %convolution_bitcast_fusion.lines_ref, s32[512,1]{1,0:T(8,128)S(1)} %convert_add_fusion.2.rows_ref, s32[1,512]{1,0:T(1,128)S(1)} %fusion.32.cols_ref), custom_call_target="tpu_custom_call" | custom-call | tf_op jit(solution)/shard_map/pallas_call | solution.py:474
  42.4 8.7 %shard_map.240 = f32[128,768]{1,0:T(8,128)S(1)} custom-call(bf16[4,128,768]{2,1,0:T(8,128)(2,1)S(1)} %bitcast.69), custom_call_target="tpu_custom_call" | custom-call | tf_op jit(solution)/shard_map/pallas_call | solution.py:193
  52.4 0.9 copy.61
  53.3 1.1 maximum_bitcast_fusion.refs_0_
  54.4 5.7 %shard_map.241 = bf16[4,128,384]{2,1,0:T(8,128)(2,1)S(1)} custom-call(bf16[4,128,384]{2,1,0:T(8,128)(2,1)S(1)} %maximum_bitcast_fusion.refs_0_), custom_call_target="tpu_custom_call" | custom-call | tf_op jit(solution)/shard_map/pallas_call | solution.py:218
  61.1 46.7 %shard_map.242 = (bf16[8,80,384]{2,1,0:T(8,128)(2,1)S(1)}, f32[768,768]{1,0:T(8,128)S(1)}, f32[768,768]{1,0:T(8,128)S(1)}) custom-call(bf16[8,80,384]{2,1,0:T(8,128)(2,1)S(1)} %bitcast.81, bf16[768,768]{1,0:T(8,128)(2,1)S(1)} %bitcast.72, bf16[768,768]{1,0:T(8,128)(2,1)S(1)} %bitcast.73), custom_call_target="tpu_custom_call" | custom-call | tf_op jit(solution)/shard_map/pallas_call | solution.py:366
  107.8 1.4 copy-done.1
  109.2 1.4 copy-done.3
  111.2 5.7 %shard_map.243 = bf16[4,128,384]{2,1,0:T(8,128)(2,1)S(1)} custom-call(bf16[4,128,384]{2,1,0:T(8,128)(2,1)S(1)} %bitcast.83), custom_call_target="tpu_custom_call" | custom-call | tf_op jit(solution)/shard_map/pallas_call | solution.py:218
  116.9 1.1 copy.63
  118.0 2.1 %fusion.35 = (f32[1,128,4,192]{1,3,0,2:T(8,128)}, f32[1,128,4,192]{1,3,0,2:T(8,128)}) fusion(f32[2,128,4,192]{1,3,0,2:T(8,128)} %bitcast.85), kind=kLoop, calls=%fused_computation.90 | loop fusion | bytes 1572864 | tf_op jit(solution)/shard_map/slice | solution.py:649
  120.0 1.2 copy.64
  122.0 1.9 %copy.66 = f32[128,768]{1,0:T(8,128)} copy(f32[128,768]{0,1:T(8,128)} %bitcast.87) | data formatting | bytes 786432 | tf_op jit(solution)/shard_map/squeeze | solution.py:649
  123.9 1.4 multiply_reduce_fusion.1
  126.2 9.5 %shard_map.244 = bf16[4,128,768]{2,1,0:T(8,128)(2,1)S(1)} custom-call(bf16[128,768]{1,0:T(8,128)(2,1)S(1)} %fusion.34.refs_0_), custom_call_target="tpu_custom_call" | custom-call | tf_op jit(solution)/shard_map/pallas_call | solution.py:218
  135.6 1.6 convolution_convert_fusion.4
  137.4 6.0 %shard_map.245 = (bf16[512,576]{1,0:T(8,128)(2,1)S(1)}, f32[3,1024]{1,0:T(4,128)S(1)}) custom-call(bf16[512,576]{1,0:T(8,128)(2,1)S(1)} %convolution_convert_fusion.2.qkv_ref, f32[3,1024]{1,0:T(4,128)S(1)} %convolution_bitcast_fusion.lines_ref, s32[512,1]{1,0:T(8,128)S(1)} %convert_add_fusion.2.rows_ref, s32[1,512]{1,0:T(1,128)S(1)} %fusion.32.cols_ref, ...), custom_call_target="tpu_custom_call" | custom-call | tf_op jit(solution)/shard_map/pallas_call | solution.py:513
  143.4 2.3 %multiply_reduce_fusion = (f32[768]{0:T(1024)S(1)}, bf16[512,768]{1,0:T(8,128)(2,1)S(1)}) fusion(bf16[4,128,768]{2,1,0:T(8,128)(2,1)S(1)} %get-tuple-element.23, bf16[512,576]{1,0:T(8,128)(2,1)S(1)} %get-tuple-element.27, bf16[768,768]{1,0:T(8,128)(2,1)} %bitcast.80), kind=kOutput, calls=%fused_computation | convolution fusion | flops 454556928 | bytes 3148800 | tf_op jit(solution)/shard_map/dot_general | solution.py:26
  146.4 1.2 copy.68
  147.6 2.9 %convolution_convert_fusion = bf16[8,96,576]{2,1,0:T(8,128)(2,1)} fusion(bf16[8,96,512]{2,1,0:T(8,128)(2,1)} %bitcast.91, bf16[512,576]{1,0:T(8,128)(2,1)S(1)} %copy-done.9), kind=kOutput, calls=%fused_computation.1 | convolution fusion | flops 453427200 | bytes 2260992 | tf_op jit(solution)/shard_map/dot_general | solution.py:20
  151.1 0.8 copy-done.20
  152.2 29.8 %shard_map.246 = (f32[128,768]{1,0:T(8,128)S(1)}, f32[96,768]{1,0:T(8,128)S(1)}, f32[8,16,768]{2,1,0:T(8,128)S(1)}) custom-call(bf16[4,128,768]{2,1,0:T(8,128)(2,1)S(1)} %bitcast.76, bf16[8,96,768]{2,1,0:T(8,128)(2,1)S(1)} %pad_maximum_fusion.weights_in, f32[16,768]{1,0:T(8,128)S(1)} %select_maximum_fusion.small_in), custom_call_target="tpu_custom_call" | custom-call | tf_op jit(solution)/shard_map/pallas_call | solution.py:425
  182.4 1.1 fusion.19
  187.0 1.4 copy.84
  188.4 1.1 copy-done.2
  189.5 1.4 copy.85
  (123 shorter events, 16.2 us)
Async XLA Ops:
  0.6 37.0 %copy-start = (bf16[32,3]{0,1:T(4,128)(2,1)S(1)}, bf16[32,3]{0,1:T(4,128)(2,1)}, u32[]{:S(2)}) copy-start(bf16[32,3]{0,1:T(4,128)(2,1)} %param.26) | copy-start | bytes 580
  31.5 10.4 %copy-start.7 = (bf16[8,96,768]{2,1,0:T(8,128)(2,1)}, bf16[8,96,768]{2,1,0:T(8,128)(2,1)S(1)}, u32[]{:S(2)}) copy-start(bf16[8,96,768]{2,1,0:T(8,128)(2,1)S(1)} %get-tuple-element.24) | copy-start | bytes 3538948
  31.5 0.8 copy-start.31
  31.5 4.1 %copy-start.25 = (s32[959]{0:T(1024)S(1)}, s32[959]{0:T(1024)}, u32[]{:S(2)}) copy-start(s32[959]{0:T(1024)} %param.18) | copy-start | bytes 11512
  31.5 6.0 %slice-start = ((s32[959]{0:T(1024)}), s32[479]{0:T(512)S(1)}, s32[]{:S(2)}) async-start(s32[959]{0:T(1024)} %param.18), calls=%async_computation | async-start | bytes 4096 | tf_op jit(solution)/shard_map/slice | solution.py:571
  41.9 9.3 %copy-start.12 = (bf16[128,768]{1,0:T(8,128)(2,1)S(1)}, bf16[128,768]{1,0:T(8,128)(2,1)}, u32[]{:S(2)}) copy-start(bf16[128,768]{1,0:T(8,128)(2,1)} %param.15) | copy-start | bytes 589828
  42.4 9.0 %copy-start.30 = (bf16[768]{0:T(1024)(128)(2,1)S(1)}, bf16[768]{0:T(1024)(128)(2,1)}, u32[]{:S(2)}) copy-start(bf16[768]{0:T(1024)(128)(2,1)} %param.20) | copy-start | bytes 4612
  42.4 9.4 %copy-start.23 = (s32[512,1]{0,1:T(1,128)S(1)}, s32[512,1]{0,1:T(1,128)}, u32[]{:S(2)}) copy-start(s32[512,1]{0,1:T(1,128)} %param.17) | copy-start | bytes 6148
  42.4 9.4 %copy-start.18 = (bf16[128,768]{1,0:T(8,128)(2,1)S(1)}, bf16[128,768]{1,0:T(8,128)(2,1)}, u32[]{:S(2)}) copy-start(bf16[128,768]{1,0:T(8,128)(2,1)} %param.29) | copy-start | bytes 589828
  51.3 74.0 %copy-start.10 = (f32[128,768]{1,0:T(8,128)}, f32[128,768]{1,0:T(8,128)S(1)}, u32[]{:S(2)}) copy-start(f32[128,768]{1,0:T(8,128)S(1)} %get-tuple-element.75) | copy-start | bytes 1179652
  51.3 74.0 %copy-start.21 = (f32[128]{0:T(128)}, f32[128]{0:T(128)S(1)}, u32[]{:S(2)}) copy-start(f32[128]{0:T(128)S(1)} %add_rsqrt_fusion) | copy-start | bytes 1540
  54.4 6.7 %copy-start.5 = (bf16[1,768,768]{2,1,0:T(8,128)(2,1)S(1)}, bf16[1,768,768]{2,1,0:T(8,128)(2,1)}, u32[]{:S(2)}) copy-start(bf16[1,768,768]{2,1,0:T(8,128)(2,1)} %param.27) | copy-start | bytes 3538948
  54.4 6.7 %copy-start.6 = (bf16[1,768,768]{2,1,0:T(8,128)(2,1)S(1)}, bf16[1,768,768]{2,1,0:T(8,128)(2,1)}, u32[]{:S(2)}) copy-start(bf16[1,768,768]{2,1,0:T(8,128)(2,1)} %param.28) | copy-start | bytes 3538948
  107.8 1.4 copy-start.1
  109.2 1.4 copy-start.3
  121.2 0.7 copy-start.16
  125.2 0.8 copy-start.14
  125.3 11.9 %copy-start.28 = (f32[128]{0:T(128)}, f32[128]{0:T(128)S(1)}, u32[]{:S(2)}) copy-start(f32[128]{0:T(128)S(1)} %broadcast_multiply_fusion.2) | copy-start | bytes 1540
  143.4 2.3 %copy-start.8 = (bf16[512,576]{1,0:T(8,128)(2,1)}, bf16[512,576]{1,0:T(8,128)(2,1)S(1)}, u32[]{:S(2)}) copy-start(bf16[512,576]{1,0:T(8,128)(2,1)S(1)} %get-tuple-element.27) | copy-start | bytes 1769476
  143.4 2.3 %copy-start.24 = (bf16[768]{0:T(1024)(128)(2,1)S(1)}, bf16[768]{0:T(1024)(128)(2,1)}, u32[]{:S(2)}) copy-start(bf16[768]{0:T(1024)(128)(2,1)} %param.19) | copy-start | bytes 4612
  145.7 1.9 copy-start.9
  150.7 1.2 copy-start.20
  152.2 29.9 %copy-start.13 = (bf16[128,768]{1,0:T(8,128)(2,1)S(1)}, bf16[128,768]{1,0:T(8,128)(2,1)}, u32[]{:S(2)}) copy-start(bf16[128,768]{1,0:T(8,128)(2,1)} %param.15) | copy-start | bytes 589828
  152.2 29.9 %copy-start.27 = (f32[128]{0:T(128)S(1)}, f32[128]{0:T(128)}, u32[]{:S(2)}) copy-start(f32[128]{0:T(128)} %copy-done.26) | copy-start | bytes 1540
  152.2 30.1 %copy-start.11 = (f32[128,768]{1,0:T(8,128)S(1)}, f32[128,768]{1,0:T(8,128)}, u32[]{:S(2)}) copy-start(f32[128,768]{1,0:T(8,128)} %copy-done.10) | copy-start | bytes 1179652
  152.2 30.1 %copy-start.15 = (f32[128,768]{1,0:T(8,128)S(1)}, f32[128,768]{1,0:T(8,128)}, u32[]{:S(2)}) copy-start(f32[128,768]{1,0:T(8,128)} %copy-done.14) | copy-start | bytes 1179652
  152.2 30.1 %copy-start.17 = (f32[128,768]{1,0:T(8,128)S(1)}, f32[128,768]{1,0:T(8,128)}, u32[]{:S(2)}) copy-start(f32[128,768]{1,0:T(8,128)} %copy-done.16) | copy-start | bytes 1179652
  152.2 30.1 %copy-start.19 = (bf16[128,768]{1,0:T(8,128)(2,1)S(1)}, bf16[128,768]{1,0:T(8,128)(2,1)}, u32[]{:S(2)}) copy-start(bf16[128,768]{1,0:T(8,128)(2,1)} %param.29) | copy-start | bytes 589828
  152.2 30.1 %copy-start.22 = (f32[128]{0:T(128)S(1)}, f32[128]{0:T(128)}, u32[]{:S(2)}) copy-start(f32[128]{0:T(128)} %copy-done.21) | copy-start | bytes 1540
  152.2 30.1 %copy-start.29 = (f32[128]{0:T(128)S(1)}, f32[128]{0:T(128)}, u32[]{:S(2)}) copy-start(f32[128]{0:T(128)} %copy-done.28) | copy-start | bytes 1540
  182.4 4.6 %copy-start.4 = (f32[768,768]{1,0:T(8,128)S(1)}, f32[768,768]{1,0:T(8,128)}, u32[]{:S(2)}) copy-start(f32[768,768]{1,0:T(8,128)} %copy-done.3) | copy-start | bytes 7077892
  187.0 2.5 %copy-start.2 = (f32[768,768]{1,0:T(8,128)S(1)}, f32[768,768]{1,0:T(8,128)}, u32[]{:S(2)}) copy-start(f32[768,768]{1,0:T(8,128)} %copy-done.1) | copy-start | bytes 7077892
  (1 other events, 0.5 us)

commit v3 on v2

--- a/solution.py
+++ b/solution.py
@@ -520,6 +520,190 @@
         out_specs=[pl.BlockSpec(memory_space=pltpu.VMEM)] * 2,
         compiler_params=pltpu.CompilerParams(vmem_limit_bytes=VMEM_BYTES),
     )(qkv, lines, seg_rows, seg_cols, grad_heads)
+
+
+def attend_and_sum(number, qkv, lines, seg_rows, seg_cols, out_part, router_part):
+    tokens, heads = qkv.shape[0], lines.shape[0]
+    width = heads * DH
+    size, ranks = lax.axis_size("dp"), lax.axis_size("tensor")
+    rows = out_part.shape[0]
+    model = size * rows
+    half_type = jnp.bfloat16
+    block = (tokens // ranks, model)
+    move = Reduce("tensor", block, half_type)
+    gather_o, gather_r = Gather("dp"), Gather("dp")
+
+    def kernel(
+        qkv_ref, lines_ref, rows_ref, cols_ref, out_in, router_in,
+        heads_out, sum_out, out_all, router_all, part, slots, sems, sems_o, sems_r,
+    ):
+        greet(("dp", "tensor"))
+        gather_o.start(out_in, out_all, sems_o)
+        gather_r.start(router_in, router_all, sems_r)
+        parts = []
+        for head in range(heads):
+            lo = head * DH
+            probs = head_probs(
+                qkv_ref[:, lo : lo + DH],
+                qkv_ref[:, width + lo : width + lo + DH],
+                lines_ref[head : head + 1, :],
+                rows_ref[...],
+                cols_ref[...],
+            )
+            values = qkv_ref[:, 2 * width + lo : 2 * width + lo + DH]
+            parts.append(matmul(probs.astype(half_type), values).astype(half_type))
+            if head == 0:
+                gather_o.middle()
+                gather_r.middle()
+        heads_out[...] = jnp.concatenate(parts, axis=1)
+        gather_o.finish()
+        gather_r.finish()
+        projected = contract_cols(heads_out[...], out_all[...].reshape(model, width))
+        part[...] = projected.astype(half_type).reshape((ranks,) + block)
+        move.start(part, slots, sems)
+        move.middle()
+        move.finish(sum_out)
+
+    return pl.pallas_call(
+        kernel,
+        out_shape=[
+            jax.ShapeDtypeStruct((tokens, width), half_type),
+            jax.ShapeDtypeStruct(block, jnp.float32),
+            jax.ShapeDtypeStruct((size,) + out_part.shape, half_type),
+            jax.ShapeDtypeStruct((size,) + router_part.shape, half_type),
+        ],
+        in_specs=[pl.BlockSpec(memory_space=pltpu.VMEM)] * 6,
+        out_specs=[pl.BlockSpec(memory_space=pltpu.VMEM)] * 4,
+        scratch_shapes=[pltpu.VMEM((ranks,) + block, half_type)]
+        + move.scratch()
+        + [gather_o.sems(), gather_r.sems()],
+        compiler_params=pltpu.CompilerParams(
+            collective_id=number, has_side_effects=True, vmem_limit_bytes=VMEM_BYTES
+        ),
+    )(qkv, lines, seg_rows, seg_cols, out_part, router_part)
+
+
+def back_and_sum(
+    number, qkv, lines, seg_rows, seg_cols, grad_attn, head_out, out_all, full_one, qkv_all,
+    sums_hot, small, gain_row,
+):
+    tokens, heads = qkv.shape[0], lines.shape[0]
+    width = heads * DH
+    size, ranks = lax.axis_size("dp"), lax.axis_size("tensor")
+    model = full_one.shape[1]
+    rows = model // size
+    buckets = sums_hot.shape[0]
+    half_type, float_type = jnp.bfloat16, jnp.float32
+    block = (tokens // ranks, model)
+    sum_t = Reduce("tensor", block, half_type)
+    sum_w = Reduce("dp", (rows, 3 * width), half_type)
+    sum_o = Reduce("dp", (rows, width), half_type)
+    gather_t, gather_d = Gather("tensor"), Gather("dp")
+
+    def kernel(
+        qkv_ref, lines_ref, rows_ref, cols_ref, attn_ref, heads_ref, out_ref, one_ref, all_ref,
+        hot_ref, small_ref, gain_ref,
+        rows_out, weights_out, proj_out, small_out,
+        norm_src, weight_src, proj_src, small_src, held, total,
+        slots_t, sems_t, slots_w, sems_w, slots_o, sems_o, sems_g, sems_h,
+    ):
+        rank = lax.axis_index("tensor")
+        greet(("dp", "tensor"))
+        grad_proj = contract_rows(attn_ref[...], heads_ref[...]).astype(half_type)
+        proj_src[...] = grad_proj.reshape(size, rows, width)
+        sum_o.start(proj_src, slots_o, sems_o)
+        grad_heads = matmul(attn_ref[...], out_ref[...]).astype(half_type)
+        row = lax.broadcasted_iota(jnp.int32, (tokens, tokens), 0)
+        col = lax.broadcasted_iota(jnp.int32, (tokens, tokens), 1)
+        flip = (row + col == tokens - 1).astype(float_type).astype(half_type)
+        grads_q, grads_k, grads_v, sums = [], [], [], []
+        for head in range(heads):
+            lo = head * DH
+            queries = qkv_ref[:, lo : lo + DH]
+            keys = qkv_ref[:, width + lo : width + lo + DH]
+            values = qkv_ref[:, 2 * width + lo : 2 * width + lo + DH]
+            grad = grad_heads[:, lo : lo + DH]
+            probs = head_probs(
+                queries, keys, lines_ref[head : head + 1, :], rows_ref[...], cols_ref[...]
+            )
+            grads_v.append(contract_rows(probs.astype(half_type), grad))
+            grad_probs = contract_cols(grad, values)
+            mean = jnp.sum(probs * grad_probs, axis=-1, keepdims=True)
+            grad_scores = (probs * (grad_probs - mean)).astype(half_type)
+            grads_q.append(matmul(grad_scores, keys) * DH ** (-0.5))
+            grads_k.append(contract_rows(grad_scores, queries) * DH ** (-0.5))
+            flipped = matmul(flip, grad_scores)
+            padded = jnp.concatenate([flipped, jnp.zeros_like(flipped)], axis=1)
+            lined = pltpu.roll(padded, 0, 1, stride=1, stride_axis=0)
+            sums.append(jnp.sum(lined, axis=0, keepdims=True))
+            if head == 0:
+                sum_o.middle()
+        grad_qkv = jnp.concatenate(grads_q + grads_k + grads_v, axis=1).astype(half_type)
+        grad_weights = contract_rows(one_ref[...], grad_qkv).astype(half_type)
+        weight_src[...] = grad_weights.reshape(size, rows, 3 * width)
+        sum_w.start(weight_src, slots_w, sems_w)
+        grad_one = contract_cols(grad_qkv, all_ref[...])
+        norm_src[...] = grad_one.astype(half_type).reshape((ranks,) + block)
+        sum_t.start(norm_src, slots_t, sems_t)
+        gain_part = jnp.sum(grad_one * one_ref[...].astype(float_type), axis=0, keepdims=True)
+        bias = [
+            jnp.sum(hot_ref[...] * line, axis=1, keepdims=True) for line in sums
+        ]
+        lane = lax.broadcasted_iota(jnp.int32, (buckets, model), 1)
+        bucket = lax.broadcasted_iota(jnp.int32, (buckets, model), 0)
+        spread = jnp.zeros((buckets, model), float_type)
+        for head in range(heads):
+            spread = spread + jnp.where(lane == bucket + head * buckets, bias[head], 0.0)
+        bias_row = jnp.sum(spread, axis=0, keepdims=True)
+        small_src[...] = small_ref[...]
+        small_src[0:1, :] = gain_part / gain_ref[...]
+        for place in range(ranks):
+            small_src[2 + place : 3 + place, :] = jnp.where(rank == place, bias_row, 0.0)
+        gather_t.start(small_src, held, sems_g)
+        sum_t.middle()
+        gather_t.middle()
+        gather_t.finish()
+        summed = held[0]
+        for place in range(1, ranks):
+            summed = summed + held[place]
+        total[...] = summed
+        gather_d.start(total, small_out, sems_h)
+        sum_w.middle()
+        sum_t.finish(rows_out)
+        gather_d.middle()
+        sum_o.finish(proj_out)
+        sum_w.finish(weights_out)
+        gather_d.finish()
+
+    return pl.pallas_call(
+        kernel,
+        out_shape=[
+            jax.ShapeDtypeStruct(block, float_type),
+            jax.ShapeDtypeStruct((rows, 3 * width), float_type),
+            jax.ShapeDtypeStruct((rows, width), float_type),
+            jax.ShapeDtypeStruct((size,) + small.shape, float_type),
+        ],
+        in_specs=[pl.BlockSpec(memory_space=pltpu.VMEM)] * 12,
+        out_specs=[pl.BlockSpec(memory_space=pltpu.VMEM)] * 4,
+        scratch_shapes=[
+            pltpu.VMEM((ranks,) + block, half_type),
+            pltpu.VMEM((size, rows, 3 * width), half_type),
+            pltpu.VMEM((size, rows, width), half_type),
+            pltpu.VMEM(small.shape, float_type),
+            pltpu.VMEM((ranks,) + small.shape, float_type),
+            pltpu.VMEM(small.shape, float_type),
+        ]
+        + sum_t.scratch()
+        + sum_w.scratch()
+        + sum_o.scratch()
+        + [gather_t.sems(), gather_d.sems()],
+        compiler_params=pltpu.CompilerParams(
+            collective_id=number, has_side_effects=True, vmem_limit_bytes=VMEM_BYTES
+        ),
+    )(
+        qkv, lines, seg_rows, seg_cols, grad_attn, head_out, out_all, full_one, qkv_all,
+        sums_hot, small, gain_row,
+    )
 
 
 def shards(
@@ -579,7 +763,9 @@
     inv_one = lax.rsqrt(jnp.mean(input_f * input_f, axis=-1, keepdims=True) + EPS)
     unit_one = input_f * inv_one
     normed_one = (unit_one * gain_one).astype(half_type)
-    packed = jnp.concatenate([w_query, w_key, w_value, w_attn_out.T], axis=1)
+    whole_rows = row_pad == row_dev
+    packed = [w_query, w_key, w_value] if whole_rows else [w_query, w_key, w_value, w_attn_out.T]
+    packed = jnp.concatenate(packed, axis=1)
     packed = jnp.pad(packed, ((0, row_pad - row_dev), (0, 0)))
     pack_cols = packed.shape[1]
     router_rows = round_up(experts, 16)
@@ -587,28 +773,35 @@
     router_part = jnp.pad(
         w_router.T, ((0, router_rows - experts), (0, router_cols - row_dev))
     )
-    packed_all, router_all, full_one = transfer(
+    early = [] if whole_rows else [router_part]
+    gathered = transfer(
         0,
         ("dp", "tensor"),
-        [Gather("dp"), Gather("dp"), Gather("tensor")],
-        [packed, router_part, normed_one],
-        [
-            (groups, row_pad, pack_cols),
-            (groups, router_rows, router_cols),
-            (ranks, tok_dev, width),
-        ],
-    )
-    packed_all = packed_all[:, :row_dev].reshape(width, pack_cols)
-    qkv_all, out_all = packed_all[:, : 3 * head_cols], packed_all[:, 3 * head_cols :]
+        [Gather("dp")] + [Gather("dp") for _ in early] + [Gather("tensor")],
+        [packed] + early + [normed_one],
+        [(groups, row_pad, pack_cols)]
+        + [(groups, router_rows, router_cols) for _ in early]
+        + [(ranks, tok_dev, width)],
+    )
+    packed_all = gathered[0][:, :row_dev].reshape(width, pack_cols)
+    qkv_all = packed_all[:, : 3 * head_cols]
+    full_one = gathered[-1].reshape(group_tok, width)
+
+    qkv = matmul(full_one, qkv_all).astype(half_type)
+    if whole_rows:
+        head_out, attn_rows, out_all, router_all = attend_and_sum(
+            1, qkv, lines, seg_rows, seg_cols, w_attn_out.T, router_part
+        )
+        out_all = out_all.reshape(width, head_cols)
+    else:
+        out_all, router_all = packed_all[:, 3 * head_cols :], gathered[1]
+        head_out = attend(qkv, lines, seg_rows, seg_cols)
+        attn_part = contract_cols(head_out, out_all).astype(half_type)
+        attn_rows = sum_rows(1, attn_part.reshape(ranks, tok_dev, width))
     router_all = jnp.transpose(router_all[:, :experts, :row_dev], (1, 0, 2)).reshape(
         experts, width
     )
-    full_one = full_one.reshape(group_tok, width)
-
-    qkv = matmul(full_one, qkv_all).astype(half_type)
-    head_out = attend(qkv, lines, seg_rows, seg_cols)
-    attn_part = contract_cols(head_out, out_all).astype(half_type)
-    mixed = input_f + sum_rows(1, attn_part.reshape(ranks, tok_dev, width))
+    mixed = input_f + attn_rows
 
     gain_two = gain_moe.astype(float_type)
     inv_two = lax.rsqrt(jnp.mean(mixed * mixed, axis=-1, keepdims=True) + EPS)
@@ -662,34 +855,51 @@
         [grad_mixed.astype(half_type)],
         [(ranks, tok_dev, width)],
     )[0].reshape(group_tok, width)
-    grad_out_proj = contract_rows(grad_attn, head_out)
-    grad_heads = matmul(grad_attn, out_all).astype(half_type)
-    grad_qkv, line_sums = attend_back(qkv, lines, seg_rows, seg_cols, grad_heads)
     sums_hot = jnp.roll(line_hot, group_tok - 1, axis=1).astype(float_type)
-    grad_bucket = lax.dot_general(
-        line_sums, sums_hot, (((1,), (1,)), ((), ())), precision=lax.Precision.HIGHEST
-    )
-    grad_full_one = contract_cols(grad_qkv, qkv_all)
-    gain_one_part = jnp.sum(grad_full_one * full_one.astype(float_type), axis=0) / gain_one
-    grad_weights = jnp.concatenate(
-        [contract_rows(full_one, grad_qkv), grad_out_proj], axis=1
-    ).astype(half_type)
-    grad_weights = jnp.pad(
-        grad_weights.reshape(groups, row_dev, pack_cols),
-        ((0, 0), (0, row_pad - row_dev), (0, 0)),
-    )
-    bias_flat = grad_bucket.reshape(1, local_heads * buckets)
-    bias_row = jnp.pad(bias_flat, ((0, 0), (0, width - local_heads * buckets)))
-    own_rank = (jnp.arange(ranks, dtype=jnp.int32) == tensor_rank).astype(float_type)
-    small = jnp.concatenate(
-        [gain_one_part[None], gain_two_part[None], own_rank[:, None] * bias_row, grad_router]
-    )
-    small = jnp.pad(small, ((0, round_up(small.shape[0], 8) - small.shape[0]), (0, 0)))
-    grad_norm_one, weight_sums, small_parts = last_sums(
-        7, grad_full_one.astype(half_type).reshape(ranks, tok_dev, width), grad_weights, small
-    )
+    if whole_rows:
+        small = jnp.concatenate(
+            [
+                jnp.zeros((1, width), float_type),
+                gain_two_part[None],
+                jnp.zeros((ranks, width), float_type),
+                grad_router,
+            ]
+        )
+        small = jnp.pad(small, ((0, round_up(small.shape[0], 8) - small.shape[0]), (0, 0)))
+        grad_norm_one, weight_sums, proj_sums, small_parts = back_and_sum(
+            7, qkv, lines, seg_rows, seg_cols, grad_attn, head_out, out_all, full_one, qkv_all,
+            sums_hot, small, gain_one[None],
+        )
+    else:
+        grad_out_proj = contract_rows(grad_attn, head_out)
+        grad_heads = matmul(grad_attn, out_all).astype(half_type)
+        grad_qkv, line_sums = attend_back(qkv, lines, seg_rows, seg_cols, grad_heads)
+        grad_bucket = lax.dot_general(
+            line_sums, sums_hot, (((1,), (1,)), ((), ())), precision=lax.Precision.HIGHEST
+        )
+        grad_full_one = contract_cols(grad_qkv, qkv_all)
+        gain_one_part = jnp.sum(grad_full_one * full_one.astype(float_type), axis=0) / gain_one
+        grad_weights = jnp.concatenate(
+            [contract_rows(full_one, grad_qkv), grad_out_proj], axis=1
+        ).astype(half_type)
+        grad_weights = jnp.pad(
+            grad_weights.reshape(groups, row_dev, pack_cols),
+            ((0, 0), (0, row_pad - row_dev), (0, 0)),
+        )
+        bias_flat = grad_bucket.reshape(1, local_heads * buckets)
+        bias_row = jnp.pad(bias_flat, ((0, 0), (0, width - local_heads * buckets)))
+        own_rank = (jnp.arange(ranks, dtype=jnp.int32) == tensor_rank).astype(float_type)
+        small = jnp.concatenate(
+            [gain_one_part[None], gain_two_part[None], own_rank[:, None] * bias_row, grad_router]
+        )
+        small = jnp.pad(small, ((0, round_up(small.shape[0], 8) - small.shape[0]), (0, 0)))
+        grad_norm_one, weight_sums, small_parts = last_sums(
+            7, grad_full_one.astype(half_type).reshape(ranks, tok_dev, width), grad_weights, small
+        )
     grad_input = grad_mixed + norm_back(grad_norm_one, unit_one, inv_one, gain_one)
-    weight_sums = weight_sums[:row_dev]
+    if not whole_rows:
+        weight_sums = weight_sums[:row_dev]
+        proj_sums = weight_sums[:, 3 * head_cols :]
     small_sums = jnp.sum(small_parts, axis=0)
     router_sum = lax.dynamic_slice(
         small_sums, (2 + ranks, lax.axis_index("dp") * row_dev), (experts, row_dev)
@@ -704,7 +914,7 @@
         weight_sums[:, :head_cols],
         weight_sums[:, head_cols : 2 * head_cols],
         weight_sums[:, 2 * head_cols : 3 * head_cols],
-        weight_sums[:, 3 * head_cols :].T,
+        proj_sums.T,
         router_sum.T,
         bias_sum.T,
         grad_w_in[None],

time: 192 us -> 188 us (0.979)
  matrix products: 11.8 us -> 5.87 us
  other arithmetic: 8.69 us -> 11.2 us
    pallas_call x4 -> x2, Pallas kernels: 48.7 us -> 52.8 us  [the longest x1 32.9 us: back_and_sum(): pl.pallas_call(kernel, out_shape=[jax.ShapeDtypeStruct(block, float_type)...]
    dot_general x3 -> x1, matrix products: 2.89 us -> 0.13 us  [contract_cols(): lax.dot_general(left, right, (((1,), (1,)), ((), ())), preferred_element_...]
    pallas_call x4, Pallas kernels: 45.9 us -> 43.6 us  [transfer(): pl.pallas_call(kernel, out_shape=[jax.ShapeDtypeStruct(s, o.dtype) for s,...]
    pallas_call x1, Pallas kernels: 46.7 us -> 44.7 us  [visit_experts(): pl.pallas_call(kernel, out_shape=[jax.ShapeDtypeStruct(blocks, operand.dt...]
    dot_general x5 -> x3, matrix products: 4.14 us -> 2.49 us  [contract_rows(): lax.dot_general(left, right, (((0,), (0,)), ((), ())), preferred_element_...]
    dot_general x5 -> x4, matrix products: 4.56 us -> 3.25 us  [matmul(): return jnp.dot(left, right, preferred_element_type=jnp.float32)]
    unnamed x68 -> x94, local copies, waits for them, and re-layouts: 11 us -> 11.9 us
where the time goes in v3:
time: 188 us; the launch traced here: 187 us
  Pallas kernels  141 us (75%)
  local copies, waits for them, and re-layouts  26.1 us (14%)
  other arithmetic  11.2 us (6%)
  matrix products  5.87 us (3%)
  between operations  2.7 us (1%)
    pallas_call x1, Pallas kernels, visit_experts(): pl.pallas_call(kernel, out_shape=[jax.ShapeDtypeStruct(blocks, operand.dt...  44.7 us
    pallas_call x4, Pallas kernels, transfer(): pl.pallas_call(kernel, out_shape=[jax.ShapeDtypeStruct(s, o.dtype) for s,...  43.6 us
    pallas_call x1, Pallas kernels, back_and_sum(): pl.pallas_call(kernel, out_shape=[jax.ShapeDtypeStruct(block, float_type)...  32.9 us
    pallas_call x1, Pallas kernels, attend_and_sum(): pl.pallas_call(kernel, out_shape=[jax.ShapeDtypeStruct((tokens, width), h...  19.8 us
    unnamed x94, local copies, waits for them, and re-layouts  11.9 us
    squeeze x2, local copies, waits for them, and re-layouts, shards(): expert_y, grad_norm_two = (returned[0], returned[1])  3.83 us

profile of v3, /device:TPU:0, one launch (start us, length us, event | category | flops | bytes accessed | tf_op | source)
XLA Modules:
  0.0 186.9 jit_solution(7620664807125062716)
XLA Ops:
  0.7 0.7 convert_element_type.110
  1.4 1.1 fusion.16
  3.0 1.0 fusion.11.refs_1_
  4.1 0.9 pad_maximum_fusion.refs_0_
  5.0 22.1 %shard_map.238 = (bf16[8,96,576]{2,1,0:T(8,128)(2,1)S(1)}, bf16[4,128,768]{2,1,0:T(8,128)(2,1)S(1)}) custom-call(bf16[96,576]{1,0:T(8,128)(2,1)S(1)} %pad_maximum_fusion.refs_0_, bf16[128,768]{1,0:T(8,128)(2,1)S(1)} %fusion.11.refs_1_), custom_call_target="tpu_custom_call" | custom-call | tf_op jit(solution)/shard_map/pallas_call | solution.py:218
  27.1 0.8 convolution_convert_fusion.qkv_ref
  30.2 0.7 convert_add_fusion.2.rows_ref
  34.2 19.8 %shard_map.239 = (bf16[512,192]{1,0:T(8,128)(2,1)S(1)}, f32[128,768]{1,0:T(8,128)S(1)}, bf16[8,96,192]{2,1,0:T(8,128)(2,1)S(1)}, bf16[8,16,128]{2,1,0:T(8,128)(2,1)S(1)}) custom-call(bf16[512,576]{1,0:T(8,128)(2,1)S(1)} %convolution_convert_fusion.qkv_ref, f32[3,1024]{1,0:T(4,128)S(1)} %convolution_bitcast_fusion.lines_ref, ...), custom_call_target="tpu_custom_call" | custom-call | tf_op jit(solution)/shard_map/pallas_call | solution.py:567
  57.2 6.4 %shard_map.240 = bf16[4,128,384]{2,1,0:T(8,128)(2,1)S(1)} custom-call(bf16[4,128,384]{2,1,0:T(8,128)(2,1)S(1)} %maximum_bitcast_fusion.refs_0_), custom_call_target="tpu_custom_call" | custom-call | tf_op jit(solution)/shard_map/pallas_call | solution.py:218
  64.5 44.7 %shard_map.241 = (bf16[8,80,384]{2,1,0:T(8,128)(2,1)S(1)}, f32[768,768]{1,0:T(8,128)S(1)}, f32[768,768]{1,0:T(8,128)S(1)}) custom-call(bf16[8,80,384]{2,1,0:T(8,128)(2,1)S(1)} %bitcast.57, bf16[768,768]{1,0:T(8,128)(2,1)S(1)} %bitcast.51, bf16[768,768]{1,0:T(8,128)(2,1)S(1)} %bitcast.52), custom_call_target="tpu_custom_call" | custom-call | tf_op jit(solution)/shard_map/pallas_call | solution.py:366
  109.2 1.4 copy-done.1
  111.2 5.7 %shard_map.242 = bf16[4,128,384]{2,1,0:T(8,128)(2,1)S(1)} custom-call(bf16[4,128,384]{2,1,0:T(8,128)(2,1)S(1)} %bitcast.59), custom_call_target="tpu_custom_call" | custom-call | tf_op jit(solution)/shard_map/pallas_call | solution.py:218
  116.9 0.7 copy-done.2
  117.7 2.1 %copy.53 = f32[4,128,384]{1,2,0:T(8,128)} copy(bf16[4,128,384]{2,1,0:T(8,128)(2,1)} %copy-done.2) | data formatting | bytes 1179648 | tf_op jit(solution)/shard_map/convert_element_type | solution.py:841
  119.8 2.1 %fusion.26 = (f32[1,128,4,192]{1,3,0,2:T(8,128)}, f32[1,128,4,192]{1,3,0,2:T(8,128)}) fusion(f32[2,128,4,192]{1,3,0,2:T(8,128)} %bitcast.64), kind=kLoop, calls=%fused_computation.67 | loop fusion | bytes 1572864 | tf_op jit(solution)/shard_map/slice | solution.py:842
  121.8 1.9 %copy.54 = f32[128,768]{1,0:T(8,128)} copy(f32[128,768]{0,1:T(8,128)} %bitcast.66) | data formatting | bytes 786432 | tf_op jit(solution)/shard_map/squeeze | solution.py:842
  123.7 1.2 fusion.18
  125.4 1.7 fusion.31
  127.1 1.9 %copy.56 = f32[128,768]{1,0:T(8,128)} copy(f32[128,768]{0,1:T(8,128)} %bitcast.65) | data formatting | bytes 786432 | tf_op jit(solution)/shard_map/squeeze | solution.py:842
  129.0 1.6 multiply_reduce_fusion
  130.8 1.0 pad_maximum_fusion.1
  131.8 0.8 fusion.25.refs_0_
  132.6 9.5 %shard_map.243 = bf16[4,128,768]{2,1,0:T(8,128)(2,1)S(1)} custom-call(bf16[128,768]{1,0:T(8,128)(2,1)S(1)} %fusion.25.refs_0_), custom_call_target="tpu_custom_call" | custom-call | tf_op jit(solution)/shard_map/pallas_call | solution.py:218
  142.5 32.9 %shard_map.244 = (f32[128,768]{1,0:T(8,128)S(1)}, f32[96,576]{1,0:T(8,128)S(1)}, f32[96,192]{1,0:T(8,128)S(1)}, f32[8,16,768]{2,1,0:T(8,128)S(1)}) custom-call(bf16[512,576]{1,0:T(8,128)(2,1)S(1)} %convolution_convert_fusion.qkv_ref, f32[3,1024]{1,0:T(4,128)S(1)} %copy-done.14, s32[512,1]{1,0:T(8,128)S(1)} %convert_add_fusion.2.rows_ref, ...), custom_call_target="tpu_custom_call" | custom-call | tf_op jit(solution)/shard_map/pallas_call | solution.py:678
  175.7 1.1 fusion.15
  176.8 0.8 fusion.27
  177.6 1.6 copy.57
  179.2 1.0 reduce_sum.102
  180.3 0.7 dynamic-slice_bitcast_fusion
  181.0 0.7 reshape_squeeze.3
  182.2 3.2 %copy.62 = f32[1,768,768]{2,1,0:T(8,128)} copy(f32[1,768,768]{2,1,0:T(8,128)} %bitcast.50) | data formatting | bytes 4718592
  185.5 1.4 copy.63
  (137 shorter events, 11.0 us)
Async XLA Ops:
  0.6 32.9 %copy-start = (bf16[32,3]{0,1:T(4,128)(2,1)S(1)}, bf16[32,3]{0,1:T(4,128)(2,1)}, u32[]{:S(2)}) copy-start(bf16[32,3]{0,1:T(4,128)(2,1)} %param.26) | copy-start | bytes 580
  27.1 1.2 copy-start.7
  27.1 1.2 copy-start.44
  27.1 4.4 %copy-start.38 = (s32[959]{0:T(1024)S(1)}, s32[959]{0:T(1024)}, u32[]{:S(2)}) copy-start(s32[959]{0:T(1024)} %param.18) | copy-start | bytes 11512
  27.1 6.4 %slice-start = ((s32[959]{0:T(1024)}), s32[479]{0:T(512)S(1)}, s32[]{:S(2)}) async-start(s32[959]{0:T(1024)} %param.18), calls=%async_computation | async-start | bytes 4096 | tf_op jit(solution)/shard_map/slice | solution.py:755
  27.1 6.6 %copy-start.27 = (bf16[192,96]{1,0:T(8,128)(2,1)S(1)}, bf16[192,96]{1,0:T(8,128)(2,1)}, u32[]{:S(2)}) copy-start(bf16[192,96]{1,0:T(8,128)(2,1)} %param.24) | copy-start | bytes 110596
  27.1 7.1 %copy-start.43 = (bf16[96,8]{0,1:T(8,128)(2,1)S(1)}, bf16[96,8]{0,1:T(8,128)(2,1)}, u32[]{:S(2)}) copy-start(bf16[96,8]{0,1:T(8,128)(2,1)} %param.25) | copy-start | bytes 4612
  28.3 25.8 %copy-start.17 = (bf16[128,768]{1,0:T(8,128)(2,1)S(1)}, bf16[128,768]{1,0:T(8,128)(2,1)}, u32[]{:S(2)}) copy-start(bf16[128,768]{1,0:T(8,128)(2,1)} %param.15) | copy-start | bytes 589828
  28.3 26.6 %copy-start.42 = (bf16[768]{0:T(1024)(128)(2,1)S(1)}, bf16[768]{0:T(1024)(128)(2,1)}, u32[]{:S(2)}) copy-start(bf16[768]{0:T(1024)(128)(2,1)} %param.20) | copy-start | bytes 4612
  33.7 21.2 %copy-start.13 = (f32[3,1024]{1,0:T(4,128)}, f32[3,1024]{1,0:T(4,128)S(1)}, u32[]{:S(2)}) copy-start(f32[3,1024]{1,0:T(4,128)S(1)} %convolution_bitcast_fusion.lines_ref) | copy-start | bytes 36868
  34.2 21.7 %copy-start.36 = (s32[512,1]{0,1:T(1,128)S(1)}, s32[512,1]{0,1:T(1,128)}, u32[]{:S(2)}) copy-start(s32[512,1]{0,1:T(1,128)} %param.17) | copy-start | bytes 6148
  34.2 21.8 %copy-start.21 = (bf16[128,768]{1,0:T(8,128)(2,1)S(1)}, bf16[128,768]{1,0:T(8,128)(2,1)}, u32[]{:S(2)}) copy-start(bf16[128,768]{1,0:T(8,128)(2,1)} %param.29) | copy-start | bytes 589828
  55.0 2.2 %copy-start.20 = (bf16[128,768]{1,0:T(8,128)(2,1)}, bf16[128,768]{1,0:T(8,128)(2,1)S(1)}, u32[]{:S(2)}) copy-start(bf16[128,768]{1,0:T(8,128)(2,1)S(1)} %multiply_convert_fusion) | copy-start | bytes 589828
  57.2 7.3 %copy-start.3 = (bf16[1,768,768]{2,1,0:T(8,128)(2,1)S(1)}, bf16[1,768,768]{2,1,0:T(8,128)(2,1)}, u32[]{:S(2)}) copy-start(bf16[1,768,768]{2,1,0:T(8,128)(2,1)} %param.27) | copy-start | bytes 3538948
  57.2 7.3 %copy-start.4 = (bf16[1,768,768]{2,1,0:T(8,128)(2,1)S(1)}, bf16[1,768,768]{2,1,0:T(8,128)(2,1)}, u32[]{:S(2)}) copy-start(bf16[1,768,768]{2,1,0:T(8,128)(2,1)} %param.28) | copy-start | bytes 3538948
  109.2 1.4 copy-start.1
  129.0 2.8 %copy-start.16 = (f32[128,768]{1,0:T(8,128)S(1)}, f32[128,768]{1,0:T(8,128)}, u32[]{:S(2)}) copy-start(f32[128,768]{1,0:T(8,128)} %copy-done.15) | copy-start | bytes 1179652
  129.0 2.8 %copy-start.22 = (bf16[128,768]{1,0:T(8,128)(2,1)S(1)}, bf16[128,768]{1,0:T(8,128)(2,1)}, u32[]{:S(2)}) copy-start(bf16[128,768]{1,0:T(8,128)(2,1)} %param.29) | copy-start | bytes 589828
  130.7 11.5 %copy-start.29 = (s32[1024]{0:T(1024)S(1)}, s32[1024]{0:T(1024)}, u32[]{:S(2)}) copy-start(s32[1024]{0:T(1024)} %copy-done.28) | copy-start | bytes 12292
  130.8 11.6 %copy-start.37 = (bf16[768]{0:T(1024)(128)(2,1)S(1)}, bf16[768]{0:T(1024)(128)(2,1)}, u32[]{:S(2)}) copy-start(bf16[768]{0:T(1024)(128)(2,1)} %param.19) | copy-start | bytes 4612
  130.8 11.6 %copy-start.6 = (bf16[8,96,576]{2,1,0:T(8,128)(2,1)S(1)}, bf16[8,96,576]{2,1,0:T(8,128)(2,1)}, u32[]{:S(2)}) copy-start(bf16[8,96,576]{2,1,0:T(8,128)(2,1)} %copy-done.5) | copy-start | bytes 2654212
  130.8 11.6 %copy-start.8 = (bf16[4,128,768]{2,1,0:T(8,128)(2,1)S(1)}, bf16[4,128,768]{2,1,0:T(8,128)(2,1)}, u32[]{:S(2)}) copy-start(bf16[4,128,768]{2,1,0:T(8,128)(2,1)} %copy-done.7) | copy-start | bytes 2359300
  130.8 11.6 %copy-start.11 = (bf16[8,96,192]{2,1,0:T(8,128)(2,1)S(1)}, bf16[8,96,192]{2,1,0:T(8,128)(2,1)}, u32[]{:S(2)}) copy-start(bf16[8,96,192]{2,1,0:T(8,128)(2,1)} %copy-done.10) | copy-start | bytes 884740
  130.8 11.6 %copy-start.14 = (f32[3,1024]{1,0:T(4,128)S(1)}, f32[3,1024]{1,0:T(4,128)}, u32[]{:S(2)}) copy-start(f32[3,1024]{1,0:T(4,128)} %copy-done.13) | copy-start | bytes 36868
  142.4 33.0 %copy-start.18 = (bf16[128,768]{1,0:T(8,128)(2,1)S(1)}, bf16[128,768]{1,0:T(8,128)(2,1)}, u32[]{:S(2)}) copy-start(bf16[128,768]{1,0:T(8,128)(2,1)} %param.15) | copy-start | bytes 589828
  142.4 33.0 %copy-start.25 = (f32[768]{0:T(1024)S(1)}, f32[768]{0:T(1024)}, u32[]{:S(2)}) copy-start(f32[768]{0:T(1024)} %copy-done.24) | copy-start | bytes 9220
  142.4 33.0 %copy-start.41 = (f32[128]{0:T(128)S(1)}, f32[128]{0:T(128)}, u32[]{:S(2)}) copy-start(f32[128]{0:T(128)} %copy-done.40) | copy-start | bytes 1540
  142.5 33.2 %copy-start.19 = (f32[128,768]{1,0:T(8,128)S(1)}, f32[128,768]{1,0:T(8,128)}, u32[]{:S(2)}) copy-start(f32[128,768]{1,0:T(8,128)} %copy.54) | copy-start | bytes 1179652
  142.5 33.2 %copy-start.31 = (f32[128]{0:T(128)S(1)}, f32[128]{0:T(128)}, u32[]{:S(2)}) copy-start(f32[128]{0:T(128)} %copy-done.30) | copy-start | bytes 1540
  142.5 33.2 %copy-start.35 = (f32[128]{0:T(128)S(1)}, f32[128]{0:T(128)}, u32[]{:S(2)}) copy-start(f32[128]{0:T(128)} %copy-done.34) | copy-start | bytes 1540
  175.4 1.4 copy-start.9
  175.4 1.4 copy-start.12
  (14 other events, 9.5 us)
